TPU v7x, 128 devices: a whole 4x4x4 slice. The times are simulated.
128 devices in a mesh: dp: 4 (over y_hi, core), vocab: 32 (over x, y_lo, z).
Axes of the slice: x: 4, y: 4 (y_hi: 2, y_lo: 2; y = y_hi * 2 + y_lo), z: 4, core: 2. Of those that a mesh axis runs over, the one named last changes fastest.
Arguments:
- hidden: bfloat16 [256, 7168], P(('dp', 'vocab')), may hold values from -82 to 82
- head_weight: bfloat16 [7168, 98304], P(None, ('dp', 'vocab')), may hold values from -4 to 4
- ref_logprobs: bfloat16 [256, 98304], P(('dp', 'vocab')), may hold values from -16 to -6
- token_ids: int32 [256], replicated, may hold values from 0 to 98303
- response_mask: int32 [256], replicated, may hold values 0 or 1
- advantages: float32 [256], replicated, may hold values from -0.6 to 0.6
Outputs:
- grad_hidden: bfloat16 [256, 7168], P(('dp', 'vocab'))
- grad_head: bfloat16 [7168, 98304], P(None, ('dp', 'vocab'))
All inputs are finite; a program needn't handle non-finite values.
Results may differ from a plain program's by a relative error of at most 0.009.
Values may be sent and summed in bfloat16 or wider, within the bound.
No kernel may reach another device: no remote copies, remote signals or barrier semaphores. Data moves between devices by JAX's collectives and lax.ppermute only.
A program may use at most 128 MiB of HBM per device.

v0:
```python
import jax
import jax.numpy as jnp
from jax import lax
from jax.sharding import PartitionSpec as P

grad_scale = 256.0


def local(hidden, head_weight, ref_logprobs, token_ids, response_mask, advantages):
    full_hidden = lax.all_gather(hidden, ("dp", "vocab"), axis=0, tiled=True)
    ref_local = lax.all_to_all(
        ref_logprobs, ("dp", "vocab"), split_axis=1, concat_axis=0, tiled=True
    )
    ref_values = ref_local.astype(jnp.float32)
    logits = jnp.dot(full_hidden, head_weight, preferred_element_type=jnp.float32)
    columns = head_weight.shape[1]
    first_entry = lax.axis_index(("dp", "vocab")) * columns
    row_top = lax.pmax(jnp.max(logits, axis=1), ("dp", "vocab"))
    shifted = logits - row_top[:, None]
    scaled = jnp.exp(shifted)
    row_total, row_cross = lax.psum(
        (jnp.sum(scaled, axis=1), jnp.sum(scaled * (shifted - ref_values), axis=1)), ("dp", "vocab")
    )
    log_total = jnp.log(row_total)
    divergence = row_cross / row_total - log_total
    log_probs = shifted - log_total[:, None]
    chance = jnp.exp(log_probs)
    entries = first_entry + jnp.arange(columns, dtype=jnp.int32)
    chosen = (token_ids[:, None] == entries[None, :]).astype(jnp.float32)
    weighting = grad_scale * response_mask.astype(jnp.float32)
    grad_logits = (
        weighting[:, None]
        * (
            chance * (log_probs - ref_values - divergence[:, None])
            - advantages[:, None] * (chosen - chance)
        )
    ).astype(jnp.bfloat16)
    grad_head = lax.dot_general(
        full_hidden, grad_logits, (((0,), (0,)), ((), ())), preferred_element_type=jnp.float32
    ).astype(jnp.bfloat16)
    summed = lax.psum_scatter(
        lax.dot_general(
            grad_logits, head_weight, (((1,), (1,)), ((), ())), preferred_element_type=jnp.float32
        ),
        ("dp", "vocab"),
        scatter_dimension=0,
        tiled=True,
    )
    return (summed.astype(jnp.bfloat16), grad_head)


def solution(mesh):
    placed = (
        P(("dp", "vocab"), None),
        P(None, ("dp", "vocab")),
        P(("dp", "vocab"), None),
        P(),
        P(),
        P(),
    )
    return jax.shard_map(
        local,
        mesh=mesh,
        in_specs=placed,
        out_specs=(P(("dp", "vocab"), None), P(None, ("dp", "vocab"))),
        check_vma=False,
    )
```

profile of v0, /device:TPU:1, one launch (start us, length us, event | category | flops | bytes accessed | tf_op | source)
XLA Modules:
  0.0 616.3 jit_solution(18250563567481515111)
XLA Ops:
  7.2 0.0 all-gather.3.cloned.1.call-start
  7.2 0.7 all-gather.3.cloned.1.call-update
  7.9 11.5 %all-to-all-start = ((bf16[2,128,768]{2,0,1:T(2,128)(2,1)}), bf16[2,128,768]{2,0,1:T(2,128)(2,1)S(1)}, u32[]{:S(2)}, u32[]{:S(2)}) async-start(bf16[2,128,768]{2,0,1:T(2,128)(2,1)} %bitcast.10), calls=%async_computation | async-start | bytes 786432 | tf_op jit(solution)/shard_map/all_to_all | solution.py:11
  19.4 0.7 convert_multiply_fusion
  20.1 11.9 %all-to-all-done = bf16[2,128,768]{2,0,1:T(2,128)(2,1)S(1)} async-done(((bf16[2,128,768]{2,0,1:T(2,128)(2,1)}), bf16[2,128,768]{2,0,1:T(2,128)(2,1)S(1)}, u32[]{:S(2)}, u32[]{:S(2)}) %all-to-all-start) | async-done | bytes 393248 | tf_op jit(solution)/shard_map/all_to_all | solution.py:11
  32.0 0.3 convert_bitcast_fusion
  32.3 0.5 reshape.19
  32.8 286.3 %all-gather.3.cloned.1.call-done = bf16[128,2,7168]{2,1,0:T(2,128)(2,1)} async-done(((bf16[1,2,7168]{2,1,0:T(2,128)(2,1)}), bf16[128,2,7168]{2,1,0:T(2,128)(2,1)}) %all-gather.3.cloned.1.call-update) | async-done | bytes 3670032 | tf_op jit(solution)/shard_map/all_gather | solution.py:10
  319.1 8.4 %reshape.21 = bf16[256,7168]{1,0:T(8,128)(2,1)} reshape(bf16[128,2,7168]{2,1,0:T(2,128)(2,1)} %all-gather.3.cloned.1.call-done) | data formatting | bytes 7340032
  327.5 0.0 copy-start.1
  327.5 0.0 copy-start.2
  327.5 8.3 %fusion.3 = (f32[256]{0:T(256)S(1)}, f32[256,768]{1,0:T(8,128)S(1)}) fusion(bf16[256,7168]{1,0:T(8,128)(2,1)} %reshape.21, bf16[7168,768]{1,0:T(8,128)(2,1)} %param.7), kind=kOutput, calls=%fused_computation.12 | convolution fusion | flops 2818768640 | bytes 15467520 | tf_op jit(solution)/shard_map/dot_general | solution.py:15
  335.9 65.0 %pmax.7 = f32[256]{0:T(256)S(1)} all-reduce(f32[256]{0:T(256)S(1)} %get-tuple-element.12), channel_id=1, replica_groups=mesh['dp'=4,'vocab'=32] {'dp','vocab'}, use_global_device_ids=true, to_apply=%region_1.0 | all-reduce | flops 256 | bytes 2048 | tf_op jit(solution)/shard_map/pmax | solution.py:18
  400.9 0.4 exponential_reduce_fusion
  401.3 63.7 %all-reduce.1 = (f32[256]{0:T(256)S(1)}, f32[256]{0:T(256)S(1)}) all-reduce(f32[256]{0:T(256)S(1)} %get-tuple-element.7, f32[256]{0:T(256)S(1)} %get-tuple-element.6), channel_id=1, replica_groups=mesh['dp'=4,'vocab'=32] {'dp','vocab'}, use_global_device_ids=true, to_apply=%region_5.0 | all-reduce | flops 512 | bytes 4096 | tf_op jit(solution)/shard_map/psum | solution.py:21
  465.0 0.0 copy-done.1
  465.0 0.0 copy-done.2
  465.0 0.0 copy-start
  465.0 13.7 %fusion.1 = f32[256,7168]{1,0:T(8,128)} fusion(bf16[7168,768]{1,0:T(8,128)(2,1)} %param.7, f32[256,768]{1,0:T(8,128)S(1)} %reshape.19, f32[256,768]{1,0:T(8,128)S(1)} %get-tuple-element.13, s32[768]{0:T(1024)S(1)} %iota_add_fusion, f32[256]{0:T(256)S(1)} %copy-done.1, f32[256]{0:T(256)S(1)} %get-tuple-element.11, f32[256]{0:T(256)S(1)} %get-tuple-element.10, ...), kind=kOutput, calls=%fused_computation.10 | convolution fusion | flops 2820931584 | bytes 19932160 | tf_op jit(solution)/shard_map/dot_general | solution.py:42
  478.7 0.0 copy-done
  478.7 6.3 %fusion = bf16[7168,768]{0,1:T(8,128)(2,1)} fusion(bf16[256,7168]{1,0:T(8,128)(2,1)S(1)} %copy-done, f32[256,768]{1,0:T(8,128)S(1)} %reshape.19, f32[256,768]{1,0:T(8,128)S(1)} %get-tuple-element.13, s32[768]{0:T(1024)S(1)} %iota_add_fusion, f32[256]{0:T(256)S(1)} %copy-done.1, f32[256]{0:T(256)S(1)} %get-tuple-element.11, f32[256]{0:T(256)S(1)} %get-tuple-element.10, ...), kind=kOutput, calls=%fused_computation.1 | convolution fusion | flops 2826436608 | bytes 16262144 | tf_op jit(solution)/shard_map/dot_general | solution.py:38
  485.0 108.3 %all-reduce.3 = bf16[256,7168]{1,0:T(8,128)(2,1)} all-reduce(f32[256,7168]{1,0:T(8,128)} %fusion.1), channel_id=2, replica_groups=mesh['dp'=4,'vocab'=32] {'dp','vocab'}, use_global_device_ids=true, to_apply=%region_6.0.clone | all-reduce | flops 1835008 | bytes 11010048
  593.3 14.6 %copy.11 = bf16[7168,768]{1,0:T(8,128)(2,1)} copy(bf16[7168,768]{0,1:T(8,128)(2,1)} %fusion) | data formatting | bytes 22020096
  607.9 1.5 dynamic-slice_convert_fusion
  (2 shorter events, 0.0 us)
Async XLA Ops:
  7.2 312.0 %all-gather.3.cloned.1.call-start = ((), (), s32[]{:S(2)}) async-start(), calls=%async_computation.1 | async-start | bytes 3698688 | tf_op jit(solution)/shard_map/all_gather | solution.py:10
  7.9 24.1 %all-to-all-start = ((bf16[2,128,768]{2,0,1:T(2,128)(2,1)}), bf16[2,128,768]{2,0,1:T(2,128)(2,1)S(1)}, u32[]{:S(2)}, u32[]{:S(2)}) async-start(bf16[2,128,768]{2,0,1:T(2,128)(2,1)} %bitcast.10), calls=%async_computation | async-start | bytes 786432 | tf_op jit(solution)/shard_map/all_to_all | solution.py:11
  327.5 137.4 %copy-start.1 = (f32[256]{0:T(256)S(1)}, f32[256]{0:T(256)}, u32[]{:S(2)}) copy-start(f32[256]{0:T(256)} %param.11) | copy-start | bytes 3076
  327.5 137.4 %copy-start.2 = (s32[256]{0:T(256)S(1)}, s32[256]{0:T(256)}, u32[]{:S(2)}) copy-start(s32[256]{0:T(256)} %param.9) | copy-start | bytes 3076
  465.0 13.7 %copy-start = (bf16[256,7168]{1,0:T(8,128)(2,1)S(1)}, bf16[256,7168]{1,0:T(8,128)(2,1)}, u32[]{:S(2)}) copy-start(bf16[256,7168]{1,0:T(8,128)(2,1)} %reshape.21) | copy-start | bytes 11010052
Sparse Core Ops, SparseCore 0:
  9.7 309.3 all-gather.2
where the time goes:
time: 618 us; the launch traced here: 616 us
  waiting for transfers between devices  299 us (48%)
  blocking collectives  237 us (38%)
  matrix products  28.4 us (5%)
  local copies, waits for them, and re-layouts  25.1 us (4%)
  between operations  14.1 us (2%)
  starting transfers between devices  11.5 us (2%)
    all_gather x1, waiting for transfers between devices, local(): full_hidden = lax.all_gather(hidden, ('dp', 'vocab'), axis=0, tiled=True)  286 us
    unnamed x1, blocking collectives  108 us
    pmax x1, blocking collectives, local(): row_top = lax.pmax(jnp.max(logits, axis=1), ('dp', 'vocab'))  65 us
    psum x1, blocking collectives, local(): lax.psum((jnp.sum(scaled, axis=1), jnp.sum(scaled * (shifted - ref_values...  63.7 us
    unnamed x8, local copies, waits for them, and re-layouts  23 us
    dot_general x1, matrix products, local(): lax.dot_general(grad_logits, head_weight, (((1,), (1,)), ((), ())), prefe...  13.7 us
  transfers between devices with their start and end apart: 2, of which 2 were waited for; matrix products, arithmetic and copies ran while one was open for 0% of the time, Pallas kernels for 0%

commit v1 on v0

v1 whole, which is shorter than its diff:
```python
import functools

import jax
import jax.numpy as jnp
import numpy as np
from jax import lax
from jax.experimental import pallas as pl
from jax.experimental.pallas import tpu as pltpu
from jax.sharding import Mesh
from jax.sharding import PartitionSpec as P

grad_scale = 256.0

AXES = ("yh", "core", "x", "yl", "z")
SIZES = (2, 2, 4, 2, 4)
PEERS = 8
ROWS = 2
HALF = 128
MIB = 1 << 20


def device_at(x, y, z, core):
    return int(np.ravel_multi_index((y // 2, core, x, y % 2, z), SIZES))


PLACE = {(0, 0): 0, (1, 0): 1, (1, 1): 2, (0, 1): 3}


def chip(e, f):
    return tuple(PLACE[(e >> k) & 1, (f >> k) & 1] for k in (2, 1, 0))


def device(core, first, second):
    return device_at(*(chip(first, second) if core == 0 else chip(second, first)), core)


FIRST = [[device(c, v, s) for v in range(8)] for c in (0, 1) for s in range(8)]
SECOND = [[device(c, s, v) for v in range(8)] for c in (0, 1) for s in range(8)]
ORDER = np.array(
    [ROWS * device(c, first, second) + r for c in (0, 1) for second in range(8) for first in range(8) for r in range(ROWS)],
    np.int32,
)


def slots(core):
    out = []
    for first in range(8):
        for second in range(8):
            e, f = (first, second) if core == 0 else (second, first)
            out += [device_at(*chip(e, f), c) for c in (0, 1)]
    return out


SLOTS = np.array([slots(0), slots(1)], np.int32)


def exchange(x, groups):
    return lax.all_to_all(
        x, AXES, split_axis=0, concat_axis=0, axis_index_groups=groups, tiled=True
    )


def swap_cores(x):
    return lax.ppermute(x, "core", [(0, 1), (1, 0)])


def pack_kernel(columns, slot_ref, hidden_ref, ref_ref, out_ref):
    per_peer = 2 * PEERS

    def one(s, _):
        source = pl.multiple_of(slot_ref[s] * columns, 128)
        target = pl.multiple_of((s % per_peer) * columns, 128)
        out_ref[s // per_peer, :, pl.ds(target, columns)] = ref_ref[:, pl.ds(source, columns)]
        return 0

    lax.fori_loop(0, PEERS * per_peer, one, 0)
    rows = hidden_ref[...]
    for peer in range(PEERS):
        out_ref[peer, :, per_peer * columns :] = rows


def pack(slot, hidden, ref_logprobs, columns):
    width = 2 * PEERS * columns + hidden.shape[1]
    return pl.pallas_call(
        functools.partial(pack_kernel, columns),
        out_shape=jax.ShapeDtypeStruct((PEERS, ROWS, width), hidden.dtype),
        grid_spec=pltpu.PrefetchScalarGridSpec(
            num_scalar_prefetch=1,
            grid=(1,),
            in_specs=[
                pl.BlockSpec(hidden.shape, lambda i, s: (0, 0)),
                pl.BlockSpec(ref_logprobs.shape, lambda i, s: (0, 0)),
            ],
            out_specs=pl.BlockSpec((PEERS, ROWS, width), lambda i, s: (0, 0, 0)),
        ),
        compiler_params=pltpu.CompilerParams(vmem_limit_bytes=16 * MIB),
        name="pack",
    )(slot, hidden, ref_logprobs)


def logits_kernel(steps, core_ref, own_ref, other_ref, own_lp_ref, other_lp_ref, weight_ref, logits_ref, stats_ref):
    step = pl.program_id(0)
    weight = weight_ref[...]

    for side, x_ref in enumerate((own_ref, other_ref)):
        part = jnp.dot(x_ref[...], weight, preferred_element_type=jnp.float32)
        rows = pl.ds(side * HALF, HALF)

        @pl.when(step == 0)
        def _(part=part, rows=rows):
            logits_ref[rows, :] = part

        @pl.when(step > 0)
        def _(part=part, rows=rows):
            logits_ref[rows, :] += part

    @pl.when(step == steps - 1)
    def _():
        sides = []
        for side, lp_ref in enumerate((own_lp_ref, other_lp_ref)):
            logits = logits_ref[pl.ds(side * HALF, HALF), :]
            top = jnp.max(logits, axis=1, keepdims=True)
            shifted = logits - top
            scaled = jnp.exp(shifted)
            total = jnp.sum(scaled, axis=1, keepdims=True)
            cross = jnp.sum(scaled * (shifted - lp_ref[...].astype(jnp.float32)), axis=1, keepdims=True)
            lane = lax.broadcasted_iota(jnp.int32, (HALF, HALF), 1)
            table = jnp.where(lane == 0, top, jnp.where(lane == 1, total, cross))
            sides.append(table.T[:8, :])
        stats_ref[...] = jnp.concatenate(sides, axis=1)


def local_logits(core, own, other, weight, block=512):
    depth, columns = weight.shape
    first = 2 * columns // block
    steps = depth // block
    tokens = 2 * HALF
    x_spec = pl.BlockSpec((HALF, block), lambda k, c: (0, first + k))
    lp_spec = pl.BlockSpec((HALF, columns), lambda k, c: (0, c[0]))
    return pl.pallas_call(
        functools.partial(logits_kernel, steps),
        out_shape=(
            jax.ShapeDtypeStruct((tokens, columns), jnp.float32),
            jax.ShapeDtypeStruct((8, tokens), jnp.float32),
        ),
        grid_spec=pltpu.PrefetchScalarGridSpec(
            num_scalar_prefetch=1,
            grid=(steps,),
            in_specs=[x_spec, x_spec, lp_spec, lp_spec, pl.BlockSpec((block, columns), lambda k, c: (k, 0))],
            out_specs=(
                pl.BlockSpec((tokens, columns), lambda k, c: (0, 0)),
                pl.BlockSpec((8, tokens), lambda k, c: (0, 0)),
            ),
        ),
        compiler_params=pltpu.CompilerParams(vmem_limit_bytes=24 * MIB),
        cost_estimate=pl.CostEstimate(
            flops=2 * tokens * depth * columns, bytes_accessed=2 * depth * (columns + tokens), transcendentals=0
        ),
        name="logits",
    )(core, own, other, own, other, weight)


def hidden_grad_kernel(core_ref, logits_ref, own_lp_ref, other_lp_ref, token_ref, weight_ref, grad_ref, own_ref, other_ref):
    @pl.when(pl.program_id(0) == 0)
    def _():
        for side, lp_ref in enumerate((own_lp_ref, other_lp_ref)):
            rows = pl.ds(side * HALF, HALF)
            pad = jnp.zeros((HALF - 8, HALF), jnp.float32)
            table = jnp.concatenate([token_ref[:, side * HALF : (side + 1) * HALF], pad], axis=0).T
            top, log_total, divergence, advantage, weighting, chosen = (table[:, i : i + 1] for i in range(6))
            log_probs = (logits_ref[rows, :] - top) - log_total
            chance = jnp.exp(log_probs)
            entry = lax.broadcasted_iota(jnp.int32, log_probs.shape, 1).astype(jnp.float32)
            picked = jnp.where(entry == chosen, 1.0, 0.0)
            ref_values = lp_ref[...].astype(jnp.float32)
            grad = weighting * (chance * (log_probs - ref_values - divergence) - advantage * (picked - chance))
            grad_ref[rows, :] = grad.astype(grad_ref.dtype)

    out = lax.dot_general(
        grad_ref[...], weight_ref[...], (((1,), (1,)), ((), ())), preferred_element_type=jnp.float32
    )
    own_ref[...] = out[:HALF]
    other_ref[...] = out[HALF:].astype(other_ref.dtype)


def hidden_grad(core, logits, own, other, token, weight, block=1024):
    depth, columns = weight.shape
    tokens = logits.shape[0]
    lp_spec = pl.BlockSpec((HALF, columns), lambda k, c: (0, c[0]))
    whole = lambda shape: pl.BlockSpec(shape, lambda k, c: (0, 0))
    return pl.pallas_call(
        hidden_grad_kernel,
        out_shape=(
            jax.ShapeDtypeStruct((tokens, columns), weight.dtype),
            jax.ShapeDtypeStruct((HALF, depth), jnp.float32),
            jax.ShapeDtypeStruct((HALF, depth), weight.dtype),
        ),
        grid_spec=pltpu.PrefetchScalarGridSpec(
            num_scalar_prefetch=1,
            grid=(depth // block,),
            in_specs=[
                whole(logits.shape),
                lp_spec,
                lp_spec,
                whole(token.shape),
                pl.BlockSpec((block, columns), lambda k, c: (k, 0)),
            ],
            out_specs=(
                whole((tokens, columns)),
                pl.BlockSpec((HALF, block), lambda k, c: (0, k)),
                pl.BlockSpec((HALF, block), lambda k, c: (0, k)),
            ),
        ),
        compiler_params=pltpu.CompilerParams(vmem_limit_bytes=24 * MIB),
        cost_estimate=pl.CostEstimate(
            flops=2 * tokens * depth * columns, bytes_accessed=2 * depth * (columns + 3 * HALF), transcendentals=0
        ),
        name="hidden_grad",
    )(core, logits, own, other, token, weight)


def head_grad_kernel(own_ref, other_ref, grad_ref, out_ref):
    x = jnp.concatenate([own_ref[...], other_ref[...]], axis=0)
    out_ref[...] = lax.dot_general(
        x, grad_ref[...], (((0,), (0,)), ((), ())), preferred_element_type=jnp.float32
    ).astype(out_ref.dtype)


def head_grad(own, other, grad, depth, block=512):
    tokens, columns = grad.shape
    first = 2 * columns // block
    x_spec = pl.BlockSpec((HALF, block), lambda k: (0, first + k))
    return pl.pallas_call(
        head_grad_kernel,
        out_shape=jax.ShapeDtypeStruct((depth, columns), grad.dtype),
        grid=(depth // block,),
        in_specs=[x_spec, x_spec, pl.BlockSpec(grad.shape, lambda k: (0, 0))],
        out_specs=pl.BlockSpec((block, columns), lambda k: (k, 0)),
        compiler_params=pltpu.CompilerParams(vmem_limit_bytes=24 * MIB),
        cost_estimate=pl.CostEstimate(
            flops=2 * tokens * depth * columns, bytes_accessed=2 * depth * (columns + tokens), transcendentals=0
        ),
        name="head_grad",
    )(own, other, grad)


def local(hidden, head_weight, ref_logprobs, token_ids, response_mask, advantages):
    depth, columns = head_weight.shape
    core = lax.axis_index("core")
    core_arr = core.reshape(1).astype(jnp.int32)
    slot = jnp.where(core == 0, SLOTS[0], SLOTS[1])

    sent = pack(slot, hidden, ref_logprobs, columns)
    got = exchange(sent, FIRST).reshape(PEERS * ROWS, sent.shape[2])
    cut = 2 * PEERS * columns
    lp = got[:, :cut].reshape(PEERS * ROWS, PEERS, 2 * columns).transpose(1, 0, 2)
    rows = jnp.broadcast_to(got[None, :, cut:], (PEERS, PEERS * ROWS, depth))
    own = exchange(jnp.concatenate([lp, rows], axis=2), SECOND).reshape(HALF, 2 * columns + depth)
    other = swap_cores(own)

    logits, stats = local_logits(core_arr, own, other, head_weight)

    def turn(table):
        return jnp.where(core == 0, table, jnp.roll(table, HALF, axis=1))

    stats = turn(stats[:3]).reshape(1, 1, 3 * 2 * HALF)
    everyone = lax.all_to_all(
        jnp.broadcast_to(stats, (128,) + stats.shape[1:]), AXES, split_axis=0, concat_axis=0, tiled=True
    ).reshape(128, 3, 2 * HALF)
    tops, totals, crosses = everyone[:, 0], everyone[:, 1], everyone[:, 2]
    row_top = jnp.max(tops, axis=0)
    below = tops - row_top[None, :]
    factor = jnp.exp(below)
    row_total = jnp.sum(factor * totals, axis=0)
    row_cross = jnp.sum(factor * (crosses + below * totals), axis=0)
    log_total = jnp.log(row_total)
    divergence = row_cross / row_total - log_total

    first_entry = lax.axis_index(AXES) * columns
    chosen = (token_ids[ORDER] - first_entry).astype(jnp.float32)
    weighting = grad_scale * response_mask[ORDER].astype(jnp.float32)
    zero = jnp.zeros_like(row_top)
    token = turn(
        jnp.stack([row_top, log_total, divergence, advantages[ORDER], weighting, chosen, zero, zero])
    )

    grad, mine, theirs = hidden_grad(core_arr, logits, own, other, token, head_weight)
    grad_head = head_grad(own, other, grad, depth)

    part = (mine + swap_cores(theirs).astype(jnp.float32)).astype(hidden.dtype)
    part = exchange(part.reshape(PEERS, PEERS * ROWS, depth), SECOND)
    part = jnp.sum(part.astype(jnp.float32), axis=0).astype(hidden.dtype)
    part = exchange(part.reshape(PEERS, ROWS, depth), FIRST)
    grad_hidden = jnp.sum(part.astype(jnp.float32), axis=0).astype(hidden.dtype)
    return grad_hidden, grad_head


def solution(mesh):
    fine = Mesh(mesh.devices.reshape(SIZES), AXES)
    return jax.shard_map(
        local,
        mesh=fine,
        in_specs=(P(AXES, None), P(None, AXES), P(AXES, None), P(), P(), P()),
        out_specs=(P(AXES, None), P(None, AXES)),
        check_vma=False,
    )
```

time: 618 us -> 148 us (0.24)
  the two profiles are of different devices: /device:TPU:1 before, /device:TPU:2 now
where the time goes in v1:
time: 148 us; the launch traced here: 147 us
  blocking collectives  60 us (41%)
  Pallas kernels  33.2 us (22%)
  local copies, waits for them, and re-layouts  19.5 us (13%)
  waiting for transfers between devices  15.4 us (10%)
  starting transfers between devices  13.6 us (9%)
  other arithmetic  4.22 us (3%)
    all_to_all x3, blocking collectives, exchange(): lax.all_to_all(x, AXES, split_axis=0, concat_axis=0, axis_index_groups=gr...  60 us
    pallas_call x1, Pallas kernels, local_logits(): pl.pallas_call(functools.partial(logits_kernel, steps), out_shape=(jax.Sh...  12.7 us
    pallas_call x1, Pallas kernels, head_grad(): pl.pallas_call(head_grad_kernel, out_shape=jax.ShapeDtypeStruct((depth, c...  12.3 us
    all_to_all x1, waiting for transfers between devices, local(): lax.all_to_all(jnp.broadcast_to(stats, (128,) + stats.shape[1:]), AXES, s...  11.6 us
    unnamed x17, local copies, waits for them, and re-layouts  10.1 us
    all_to_all x1, starting transfers between devices, local(): lax.all_to_all(jnp.broadcast_to(stats, (128,) + stats.shape[1:]), AXES, s...  7.56 us
    pallas_call x1, Pallas kernels, hidden_grad(): pl.pallas_call(hidden_grad_kernel, out_shape=(jax.ShapeDtypeStruct((token...  6.17 us
    all_to_all x1, starting transfers between devices, exchange(): lax.all_to_all(x, AXES, split_axis=0, concat_axis=0, axis_index_groups=gr...  5.95 us
  transfers between devices with their start and end apart: 4, of which 2 were waited for; matrix products, arithmetic and copies ran while one was open for 4% of the time, Pallas kernels for 8%

profile of v1, /device:TPU:2, one launch (start us, length us, event | category | flops | bytes accessed | tf_op | source)
XLA Modules:
  0.0 146.8 jit_solution(14558263622714926915)
XLA Ops:
  0.7 0.7 broadcast_select_fusion.slot_ref
  1.3 1.0 copy-done.3
  2.3 0.7 copy-done.4
  3.1 2.0 %pack.1 = bf16[8,2,19456]{2,1,0:T(2,128)(2,1)S(1)} custom-call(s32[128]{0:T(128)S(1)} %broadcast_select_fusion.slot_ref, bf16[2,7168]{1,0:T(2,128)(2,1)S(1)} %copy-done.4, bf16[2,98304]{1,0:T(2,128)(2,1)S(1)} %copy-done.3), custom_call_target="tpu_custom_call" | custom-call | tf_op jit(solution)/shard_map/pack/pallas_call | solution.py:84
  5.1 12.9 %all_to_all.25 = bf16[8,2,19456]{2,1,0:T(2,128)(2,1)S(1)} all-to-all(bf16[8,2,19456]{2,1,0:T(2,128)(2,1)S(1)} %pack.1), channel_id=1, replica_groups={{0,1,4,5,8,9,12,13},{3,2,7,6,11,10,15,14},{68,69,64,65,76,77,72,73},{71..., dimensions={0} | all-to-all | bytes 1245184 | tf_op jit(solution)/shard_map/all_to_all | solution.py:58
  19.0 26.5 %all_to_all.26 = bf16[8,16,8704]{2,1,0:T(8,128)(2,1)S(1)} all-to-all(bf16[8,16,8704]{2,1,0:T(8,128)(2,1)S(1)} %pad_maximum_fusion), channel_id=1, replica_groups={{0,3,68,71,24,27,92,95},{1,2,69,70,25,26,93,94},{4,7,64,67,28,31,88,91}..., dimensions={0} | all-to-all | bytes 4456448 | tf_op jit(solution)/shard_map/all_to_all | solution.py:58
  45.5 1.9 %gather_fusion.2 = s32[256]{0:T(256)S(1)} fusion(s32[256]{0:T(256)S(1)} %copy-done, s32[1024]{0:T(1024)S(1)} %pad_clamp_fusion), kind=kCustom, calls=%fused_computation.2 | custom fusion | bytes 3072 | tf_op jit(solution)/shard_map/gather | solution.py:280
  47.4 1.9 %gather_fusion.1 = s32[256]{0:T(256)S(1)} fusion(s32[256]{0:T(256)S(1)} %copy-done.5, s32[1024]{0:T(1024)S(1)} %pad_clamp_fusion), kind=kCustom, calls=%fused_computation.1 | custom fusion | bytes 3072 | tf_op jit(solution)/shard_map/gather | solution.py:281
  49.4 1.9 %gather_fusion = f32[256]{0:T(256)S(1)} fusion(f32[256]{0:T(256)S(1)} %copy-done.6, s32[1024]{0:T(1024)S(1)} %pad_clamp_fusion), kind=kCustom, calls=%fused_computation | custom fusion | bytes 3072 | tf_op jit(solution)/shard_map/gather | solution.py:284
  51.4 4.1 %copy-done.1 = bf16[7168,768]{1,0:T(8,128)(2,1)S(1)} copy-done((bf16[7168,768]{1,0:T(8,128)(2,1)S(1)}, bf16[7168,768]{1,0:T(8,128)(2,1)}, u32[]{:S(2)}) %copy-start.1) | copy-done | bytes 11010072
  55.5 12.7 %logits.1 = (f32[256,768]{1,0:T(8,128)S(1)}, f32[8,256]{1,0:T(8,128)S(1)}) custom-call(s32[1]{0:T(128)} %bitcast.core_ref, bf16[128,8704]{1,0:T(8,128)(2,1)S(1)} %bitcast.39, bf16[128,8704]{1,0:T(8,128)(2,1)} %collective-permute-done.other_ref.other_lp_ref, bf16[128,8704]{1,0:T(8,128)(2,1)S(1)} %bitcast.40, ...), custom_call_target="tpu_custom_call" | custom-call | flops 2818572288 | bytes 14680064 | tf_op jit(solution)/shard_map/logits/pallas_call | solution.py:140
  68.2 0.9 broadcast_in_dim.25
  69.2 7.6 %all-to-all-start.2 = ((f32[128,1,768]{2,1,0:T(1,128)}), f32[128,1,768]{2,1,0:T(1,128)}, u32[]{:S(2)}, u32[]{:S(2)}) async-start(f32[128,1,768]{2,1,0:T(1,128)} %broadcast_in_dim.25), calls=%async_computation.2 | async-start | bytes 786432 | tf_op jit(solution)/shard_map/all_to_all | solution.py:267
  76.8 11.6 %all-to-all-done.2 = f32[128,1,768]{2,1,0:T(1,128)} async-done(((f32[128,1,768]{2,1,0:T(1,128)}), f32[128,1,768]{2,1,0:T(1,128)}, u32[]{:S(2)}, u32[]{:S(2)}) %all-to-all-start.2) | async-done | bytes 393248 | tf_op jit(solution)/shard_map/all_to_all | solution.py:267
  88.4 1.2 copy.22
  90.0 4.1 %copy-done.2 = bf16[7168,768]{1,0:T(8,128)(2,1)S(1)} copy-done((bf16[7168,768]{1,0:T(8,128)(2,1)S(1)}, bf16[7168,768]{1,0:T(8,128)(2,1)}, u32[]{:S(2)}) %copy-start.2) | copy-done | bytes 11010072
  94.1 6.2 %hidden_grad.1 = (bf16[256,768]{1,0:T(8,128)(2,1)S(1)}, f32[128,7168]{1,0:T(8,128)S(1)}, bf16[128,7168]{1,0:T(8,128)(2,1)S(1)}) custom-call(s32[1]{0:T(128)} %bitcast.core_ref, f32[256,768]{1,0:T(8,128)S(1)} %get-tuple-element.7.logits_ref, bf16[128,8704]{1,0:T(8,128)(2,1)S(1)} %bitcast.41, bf16[128,8704]{1,0:T(8,128)(2,1)} %collective-permute-done.other_ref.other_lp_ref, ...), custom_call_target="tpu_custom_call" | custom-call | flops 2818572288 | bytes 16515072 | tf_op jit(solution)/shard_map/hidden_grad/pallas_call | solution.py:191
  100.4 3.8 %collective-permute-done.1 = bf16[128,7168]{1,0:T(8,128)(2,1)S(1)} collective-permute-done((bf16[128,7168]{1,0:T(8,128)(2,1)S(1)}, bf16[128,7168]{1,0:T(8,128)(2,1)S(1)}, u32[]{:S(2)}, u32[]{:S(2)}) %collective-permute-start.1) | collective-permute-done | bytes 1835040 | tf_op jit(solution)/shard_map/ppermute | solution.py:64
  104.5 20.6 %all_to_all.27 = bf16[8,16,7168]{2,1,0:T(8,128)(2,1)} all-to-all(bf16[8,16,7168]{2,1,0:T(8,128)(2,1)S(1)} %bitcast.43), channel_id=1, replica_groups={{0,3,68,71,24,27,92,95},{1,2,69,70,25,26,93,94},{4,7,64,67,28,31,88,91}..., dimensions={0} | all-to-all | bytes 3670016 | tf_op jit(solution)/shard_map/all_to_all | solution.py:58
  125.2 1.8 %reduce_sum.44 = bf16[16,7168]{1,0:T(8,128)(2,1)S(1)} reduce(bf16[8,16,7168]{2,1,0:T(8,128)(2,1)} %all_to_all.27, bf16[]{:T(256)} %constant.51.clone.1), dimensions={0}, to_apply=%region_3.4 | reduce | flops 802816 | bytes 2064386 | tf_op jit(solution)/shard_map/reduce_sum | solution.py:292
  127.0 0.8 reshape.86
  127.8 5.9 %all-to-all-start.4 = ((bf16[8,2,7168]{2,1,0:T(2,128)(2,1)}), bf16[8,2,7168]{2,1,0:T(2,128)(2,1)S(1)}, u32[]{:S(2)}, u32[]{:S(2)}) async-start(bf16[8,2,7168]{2,1,0:T(2,128)(2,1)} %reshape.86), calls=%async_computation.4 | async-start | bytes 458752 | tf_op jit(solution)/shard_map/all_to_all | solution.py:58
  133.7 12.3 %head_grad.1 = bf16[7168,768]{1,0:T(8,128)(2,1)} custom-call(bf16[128,8704]{1,0:T(8,128)(2,1)S(1)} %bitcast.42, bf16[128,8704]{1,0:T(8,128)(2,1)} %collective-permute-done.other_ref.other_lp_ref, bf16[256,768]{1,0:T(8,128)(2,1)S(1)} %get-tuple-element.11.grad_ref), custom_call_target="tpu_custom_call" | custom-call | flops 2818572288 | bytes 14680064 | tf_op jit(solution)/shard_map/head_grad/pallas_call | solution.py:233
  146.0 0.8 reduce_sum.45
  (38 shorter events, 1.8 us)
Async XLA Ops:
  0.6 44.8 %copy-start = (s32[256]{0:T(256)S(1)}, s32[256]{0:T(256)}, u32[]{:S(2)}) copy-start(s32[256]{0:T(256)} %param.15) | copy-start | bytes 3076
  1.3 1.0 copy-start.3
  2.3 0.7 copy-start.4
  18.9 26.5 %copy-start.7 = (s32[256]{0:T(256)S(1)}, s32[256]{0:T(256)}, u32[]{:S(2)}) copy-start(s32[256]{0:T(256)} %constant.59) | copy-start | bytes 3076
  18.9 28.5 %copy-start.5 = (s32[256]{0:T(256)S(1)}, s32[256]{0:T(256)}, u32[]{:S(2)}) copy-start(s32[256]{0:T(256)} %param.16) | copy-start | bytes 3076
  18.9 30.5 %copy-start.6 = (f32[256]{0:T(256)S(1)}, f32[256]{0:T(256)}, u32[]{:S(2)}) copy-start(f32[256]{0:T(256)} %param.17) | copy-start | bytes 3076
  45.5 5.9 %collective-permute-start = (bf16[128,8704]{1,0:T(8,128)(2,1)S(1)}, bf16[128,8704]{1,0:T(8,128)(2,1)}, u32[]{:S(2)}, u32[]{:S(2)}) collective-permute-start(bf16[128,8704]{1,0:T(8,128)(2,1)S(1)} %bitcast.38), channel_id=1, source_target_pairs={{0,32},{32,0},{1,33},{33,1},{2,34},{34,2},{3,35},{35,3},{4,36},{36... | collective-permute-start | bytes 6684680 | tf_op jit(solution)/shard_map/ppermute | solution.py:64
  51.4 4.1 %copy-start.1 = (bf16[7168,768]{1,0:T(8,128)(2,1)S(1)}, bf16[7168,768]{1,0:T(8,128)(2,1)}, u32[]{:S(2)}) copy-start(bf16[7168,768]{1,0:T(8,128)(2,1)} %weight_ref.3) | copy-start | bytes 33030148
  69.2 19.2 %all-to-all-start.2 = ((f32[128,1,768]{2,1,0:T(1,128)}), f32[128,1,768]{2,1,0:T(1,128)}, u32[]{:S(2)}, u32[]{:S(2)}) async-start(f32[128,1,768]{2,1,0:T(1,128)} %broadcast_in_dim.25), calls=%async_computation.2 | async-start | bytes 786432 | tf_op jit(solution)/shard_map/all_to_all | solution.py:267
  90.0 4.1 %copy-start.2 = (bf16[7168,768]{1,0:T(8,128)(2,1)S(1)}, bf16[7168,768]{1,0:T(8,128)(2,1)}, u32[]{:S(2)}) copy-start(bf16[7168,768]{1,0:T(8,128)(2,1)} %weight_ref.3) | copy-start | bytes 33030148
  100.3 3.9 %collective-permute-start.1 = (bf16[128,7168]{1,0:T(8,128)(2,1)S(1)}, bf16[128,7168]{1,0:T(8,128)(2,1)S(1)}, u32[]{:S(2)}, u32[]{:S(2)}) collective-permute-start(bf16[128,7168]{1,0:T(8,128)(2,1)S(1)} %get-tuple-element.10), channel_id=1, source_target_pairs={{0,32},{32,0},{1,33},{33,1},{2,34},{34,2},{3,35},{35,3},{4,36},{36... | collective-permute-start | bytes 5505032 | tf_op jit(solution)/shard_map/ppermute | solution.py:64
  127.8 18.3 %all-to-all-start.4 = ((bf16[8,2,7168]{2,1,0:T(2,128)(2,1)}), bf16[8,2,7168]{2,1,0:T(2,128)(2,1)S(1)}, u32[]{:S(2)}, u32[]{:S(2)}) async-start(bf16[8,2,7168]{2,1,0:T(2,128)(2,1)} %reshape.86), calls=%async_computation.4 | async-start | bytes 458752 | tf_op jit(solution)/shard_map/all_to_all | solution.py:58

commit v2 on v0

v2 whole, which is shorter than its diff:
```python
import functools

import jax
import jax.numpy as jnp
import numpy as np
from jax import lax
from jax.experimental import pallas as pl
from jax.experimental.pallas import tpu as pltpu
from jax.sharding import Mesh
from jax.sharding import PartitionSpec as P

grad_scale = 256.0

AXES = ("yh", "core", "x", "yl", "z")
CHIPS = ("yh", "x", "yl", "z")
SIZES = (2, 2, 4, 2, 4)
PEERS = 8
ROWS = 2
HALF = 128
MIB = 1 << 20


def device_at(x, y, z, core):
    return int(np.ravel_multi_index((y // 2, core, x, y % 2, z), SIZES))


PLACE = {(0, 0): 0, (1, 0): 1, (1, 1): 2, (0, 1): 3}


def chip(e, f):
    return tuple(PLACE[(e >> k) & 1, (f >> k) & 1] for k in (2, 1, 0))


def device(core, first, second, to=None):
    place = chip(first, second) if core == 0 else chip(second, first)
    return device_at(*place, core if to is None else to)


FIRST = [[device(c, v, s) for v in range(8)] for c in (0, 1) for s in range(8)]
SECOND = [[device(c, s, v) for v in range(8)] for c in (0, 1) for s in range(8)]
ORDER = [
    [ROWS * device(c, first, second) + r for second in range(8) for first in range(8) for r in range(ROWS)]
    for c in (0, 1)
]
LOCAL_ORDER = np.array([ORDER[0] + ORDER[1], ORDER[1] + ORDER[0]], np.int32)


def exchange(x, groups):
    return lax.all_to_all(
        x, AXES, split_axis=0, concat_axis=0, axis_index_groups=groups, tiled=True
    )


def swap_cores(x):
    return lax.ppermute(x, "core", [(0, 1), (1, 0)])


def pack_kernel(columns, hidden_ref, ref_ref, out_ref):
    core = lax.axis_index("core")
    for mine in (0, 1):

        @pl.when(core == mine)
        def _(mine=mine):
            for first in range(PEERS):
                target = 0
                for second in range(PEERS):
                    for to in (mine, 1 - mine):
                        source = device(mine, first, second, to) * columns
                        out_ref[first, :, target : target + columns] = ref_ref[:, source : source + columns]
                        target += columns

    rows = hidden_ref[...]
    for peer in range(PEERS):
        out_ref[peer, :, 2 * PEERS * columns :] = rows


def pack(hidden, ref_logprobs, columns):
    width = 2 * PEERS * columns + hidden.shape[1]
    whole = lambda shape: pl.BlockSpec(shape, lambda i: (0,) * len(shape))
    return pl.pallas_call(
        functools.partial(pack_kernel, columns),
        out_shape=jax.ShapeDtypeStruct((PEERS, ROWS, width), hidden.dtype),
        grid=(1,),
        in_specs=[whole(hidden.shape), whole(ref_logprobs.shape)],
        out_specs=whole((PEERS, ROWS, width)),
        compiler_params=pltpu.CompilerParams(vmem_limit_bytes=8 * MIB),
        name="pack",
    )(pltpu.with_memory_space_constraint(hidden, pltpu.HBM), pltpu.with_memory_space_constraint(ref_logprobs, pltpu.HBM))


def logits_kernel(block, first, own_ref, other_ref, weight_ref, logits_ref, stats_ref):
    depth, columns = weight_ref.shape
    for step in range(depth // block):
        here = slice(first + step * block, first + (step + 1) * block)
        x = jnp.concatenate([own_ref[:, here], other_ref[:, here]], axis=0)
        part = jnp.dot(x, weight_ref[step * block : (step + 1) * block, :], preferred_element_type=jnp.float32)
        if step == 0:
            logits_ref[...] = part
        else:
            logits_ref[...] += part
    rows = []
    for side, lp_ref in enumerate((own_ref, other_ref)):
        logits = logits_ref[side * HALF : (side + 1) * HALF, :]
        lp = lp_ref[:, side * columns : (side + 1) * columns].astype(jnp.float32)
        top = jnp.max(logits, axis=1, keepdims=True)
        shifted = logits - top
        scaled = jnp.exp(shifted)
        total = jnp.sum(scaled, axis=1, keepdims=True)
        cross = jnp.sum(scaled * (shifted - lp), axis=1, keepdims=True)
        lane = lax.broadcasted_iota(jnp.int32, (HALF, HALF), 1)
        rows.append(jnp.where(lane == 0, top, jnp.where(lane == 1, total, cross)).T)
    parts = [rows[side][i : i + 1] for i in range(3) for side in (0, 1)]
    stats_ref[...] = jnp.concatenate(parts + [jnp.zeros((2, HALF), jnp.float32)], axis=0)


def local_logits(own, other, weight, block=1024):
    depth, columns = weight.shape
    tokens = 2 * HALF
    return pl.pallas_call(
        functools.partial(logits_kernel, block, 2 * columns),
        out_shape=(
            jax.ShapeDtypeStruct((tokens, columns), jnp.float32),
            jax.ShapeDtypeStruct((8, HALF), jnp.float32),
        ),
        in_specs=[pl.BlockSpec(memory_space=pltpu.VMEM)] * 3,
        out_specs=(pl.BlockSpec(memory_space=pltpu.VMEM),) * 2,
        compiler_params=pltpu.CompilerParams(vmem_limit_bytes=24 * MIB),
        cost_estimate=pl.CostEstimate(
            flops=2 * tokens * depth * columns, bytes_accessed=2 * depth * (columns + tokens), transcendentals=0
        ),
        name="logits",
    )(own, other, weight)


def merged(tops, totals, crosses):
    top = jnp.max(tops, axis=0)
    below = tops - top[None]
    factor = jnp.exp(below)
    return top, jnp.sum(factor * totals, axis=0), jnp.sum(factor * (crosses + below * totals), axis=0)


def merge_kernel(mine_ref, theirs_ref, out_ref):
    mine, theirs = mine_ref[...], theirs_ref[...]
    pair = lambda i: jnp.stack(
        [mine[2 * i : 2 * i + 2], jnp.concatenate([theirs[2 * i + 1 : 2 * i + 2], theirs[2 * i : 2 * i + 1]], axis=0)]
    )
    top, total, cross = merged(pair(0), pair(1), pair(2))
    tile = jnp.concatenate([top, total, cross, jnp.zeros_like(top)], axis=0)
    out_ref[...] = jnp.broadcast_to(tile[None], out_ref.shape)


def merge(mine, theirs, peers):
    return pl.pallas_call(
        merge_kernel,
        out_shape=jax.ShapeDtypeStruct((peers,) + mine.shape, mine.dtype),
        in_specs=[pl.BlockSpec(memory_space=pltpu.VMEM)] * 2,
        out_specs=pl.BlockSpec(memory_space=pltpu.VMEM),
        compiler_params=pltpu.CompilerParams(vmem_limit_bytes=8 * MIB),
        name="merge",
    )(mine, theirs)


def hidden_grad_kernel(block, logits_ref, own_ref, other_ref, stats_ref, token_ref, weight_ref, grad_ref, mine_ref, theirs_ref):
    depth, columns = weight_ref.shape
    stats = stats_ref[...]
    top, total, cross = merged(stats[:, 0:2], stats[:, 2:4], stats[:, 4:6])
    log_total = jnp.log(total)
    divergence = cross / total - log_total
    for side, lp_ref in enumerate((own_ref, other_ref)):
        rows = slice(side * HALF, (side + 1) * HALF)
        lines = [v[side : side + 1] for v in (top, log_total, divergence)]
        lines += [token_ref[2 * i + side : 2 * i + side + 1, :] for i in range(3)]
        pad = jnp.zeros((HALF - len(lines), HALF), jnp.float32)
        table = jnp.concatenate(lines + [pad], axis=0).T
        row_top, row_log, row_div, chosen, weighting, advantage = (table[:, i : i + 1] for i in range(6))
        log_probs = (logits_ref[rows, :] - row_top) - row_log
        chance = jnp.exp(log_probs)
        entry = lax.broadcasted_iota(jnp.int32, log_probs.shape, 1).astype(jnp.float32)
        picked = jnp.where(entry == chosen, 1.0, 0.0)
        lp = lp_ref[:, side * columns : (side + 1) * columns].astype(jnp.float32)
        grad = weighting * (chance * (log_probs - lp - row_div) - advantage * (picked - chance))
        grad_ref[rows, :] = grad.astype(grad_ref.dtype)

    for step in range(depth // block):
        here = slice(step * block, (step + 1) * block)
        out = lax.dot_general(
            grad_ref[...], weight_ref[here, :], (((1,), (1,)), ((), ())), preferred_element_type=jnp.float32
        )
        mine_ref[:, here] = out[:HALF]
        theirs_ref[:, here] = out[HALF:].astype(theirs_ref.dtype)


def hidden_grad(logits, own, other, stats, token, weight, block=1024):
    depth, columns = weight.shape
    tokens = logits.shape[0]
    return pl.pallas_call(
        functools.partial(hidden_grad_kernel, block),
        out_shape=(
            jax.ShapeDtypeStruct((tokens, columns), weight.dtype),
            jax.ShapeDtypeStruct((HALF, depth), jnp.float32),
            jax.ShapeDtypeStruct((HALF, depth), weight.dtype),
        ),
        in_specs=[pl.BlockSpec(memory_space=pltpu.VMEM)] * 6,
        out_specs=(pl.BlockSpec(memory_space=pltpu.VMEM),) * 3,
        compiler_params=pltpu.CompilerParams(vmem_limit_bytes=28 * MIB),
        cost_estimate=pl.CostEstimate(
            flops=2 * tokens * depth * columns, bytes_accessed=2 * depth * (columns + 3 * HALF), transcendentals=0
        ),
        name="hidden_grad",
    )(logits, own, other, stats, token, weight)


def head_grad_kernel(own_ref, other_ref, grad_ref, out_ref):
    x = jnp.concatenate([own_ref[...], other_ref[...]], axis=0)
    out_ref[...] = lax.dot_general(
        x, grad_ref[...], (((0,), (0,)), ((), ())), preferred_element_type=jnp.float32
    ).astype(out_ref.dtype)


def head_grad(own, other, grad, depth, block=512):
    tokens, columns = grad.shape
    first = 2 * columns // block
    x_spec = pl.BlockSpec((HALF, block), lambda k: (0, first + k))
    return pl.pallas_call(
        head_grad_kernel,
        out_shape=jax.ShapeDtypeStruct((depth, columns), grad.dtype),
        grid=(depth // block,),
        in_specs=[x_spec, x_spec, pl.BlockSpec(grad.shape, lambda k: (0, 0))],
        out_specs=pl.BlockSpec((block, columns), lambda k: (k, 0)),
        compiler_params=pltpu.CompilerParams(vmem_limit_bytes=16 * MIB),
        cost_estimate=pl.CostEstimate(
            flops=2 * tokens * depth * columns, bytes_accessed=2 * depth * (columns + tokens), transcendentals=0
        ),
        name="head_grad",
    )(own, other, grad)


def local(hidden, head_weight, ref_logprobs, token_ids, response_mask, advantages):
    depth, columns = head_weight.shape
    core = lax.axis_index("core")
    weight = pltpu.with_memory_space_constraint(head_weight, pltpu.VMEM)

    order = jnp.where(core == 0, LOCAL_ORDER[0], LOCAL_ORDER[1])
    places = lax.broadcasted_iota(jnp.int32, (2 * HALF, 2 * HALF), 0)
    arrange = lambda v: jnp.sum(jnp.where(places == order[None, :], v[:, None], 0), axis=0)
    chosen = (arrange(token_ids) - lax.axis_index(AXES) * columns).astype(jnp.float32)
    weighting = grad_scale * arrange(response_mask).astype(jnp.float32)
    token = jnp.concatenate([chosen, weighting, arrange(advantages), jnp.zeros_like(chosen)]).reshape(8, HALF)

    sent, token = lax.optimization_barrier((pack(hidden, ref_logprobs, columns), token))
    got = exchange(sent, FIRST).reshape(PEERS * ROWS, sent.shape[2])
    cut = 2 * PEERS * columns
    lp = got[:, :cut].reshape(PEERS * ROWS, PEERS, 2 * columns).transpose(1, 0, 2)
    rows = jnp.broadcast_to(got[None, :, cut:], (PEERS, PEERS * ROWS, depth))
    own = exchange(jnp.concatenate([lp, rows], axis=2), SECOND).reshape(HALF, 2 * columns + depth)
    other = swap_cores(own)

    logits, stats = local_logits(own, other, weight)
    stats = merge(stats, swap_cores(stats), 64)
    stats = lax.all_to_all(stats, CHIPS, split_axis=0, concat_axis=0, tiled=True)

    grad, mine, theirs = hidden_grad(logits, own, other, stats, token, weight)
    grad_head = head_grad(own, other, grad, depth)

    part = (mine + swap_cores(theirs).astype(jnp.float32)).astype(hidden.dtype)
    part = exchange(part.reshape(PEERS, PEERS * ROWS, depth), SECOND)
    part = jnp.sum(part.astype(jnp.float32), axis=0).astype(hidden.dtype)
    part, grad_head = lax.optimization_barrier((part.reshape(PEERS, ROWS, depth), grad_head))
    part = exchange(part, FIRST)
    grad_hidden = jnp.sum(part.astype(jnp.float32), axis=0).astype(hidden.dtype)
    return grad_hidden, grad_head


def solution(mesh):
    fine = Mesh(mesh.devices.reshape(SIZES), AXES)
    return jax.shard_map(
        local,
        mesh=fine,
        in_specs=(P(AXES, None), P(None, AXES), P(AXES, None), P(), P(), P()),
        out_specs=(P(AXES, None), P(None, AXES)),
        check_vma=False,
    )
```

time: 618 us -> 114 us (0.18)
  waiting for transfers between devices: 299 us -> 10.6 us
  blocking collectives: 237 us -> 66 us
  matrix products: 28.4 us -> 0 us
  local copies, waits for them, and re-layouts: 25.1 us -> 2.49 us
  Pallas kernels: 0 us -> 17.7 us
  between operations: 14.1 us -> 0.79 us
    all_gather x1 -> x0, waiting for transfers between devices: 286 us -> none  [local(): full_hidden = lax.all_gather(hidden, ('dp', 'vocab'), axis=0, tiled=True)]
    unnamed x1 -> x0, blocking collectives: 108 us -> none
    all_to_all x0 -> x4, blocking collectives: none -> 66 us  [the longest x3 52.8 us: exchange(): lax.all_to_all(x, AXES, split_axis=0, concat_axis=0, axis_index_groups=gr...]
    pmax x1 -> x0, blocking collectives: 65 us -> none  [local(): row_top = lax.pmax(jnp.max(logits, axis=1), ('dp', 'vocab'))]
    psum x1 -> x0, blocking collectives: 63.7 us -> none  [local(): lax.psum((jnp.sum(scaled, axis=1), jnp.sum(scaled * (shifted - ref_values...]
    dot_general x3 -> x0, matrix products: 28.4 us -> none  [the longest x1 13.7 us: local(): lax.dot_general(grad_logits, head_weight, (((1,), (1,)), ((), ())), prefe...]
    unnamed x8 -> x7, local copies, waits for them, and re-layouts: 23 us -> 1.75 us
    pallas_call x0 -> x5, Pallas kernels: none -> 17.7 us  [the longest x1 9.61 us: head_grad(): pl.pallas_call(head_grad_kernel, out_shape=jax.ShapeDtypeStruct((depth, c...]
  transfers between devices with their start and end apart: 2 -> 4, of which waited for: 2 -> 4; matrix products, arithmetic and copies ran while one was open for 0% -> 0% of each run, Pallas kernels for 0% -> 8%
where the time goes in v2:
time: 114 us
  blocking collectives  66 us (58%)
  Pallas kernels  17.7 us (16%)
  waiting for transfers between devices  10.6 us (9%)
  starting transfers between devices  9.36 us (8%)
  other arithmetic  6.79 us (6%)
  local copies, waits for them, and re-layouts  2.49 us (2%)
    all_to_all x3, blocking collectives, exchange(): lax.all_to_all(x, AXES, split_axis=0, concat_axis=0, axis_index_groups=gr...  52.8 us
    all_to_all x1, blocking collectives, local(): lax.all_to_all(stats, CHIPS, split_axis=0, concat_axis=0, tiled=True)  13.2 us
    pallas_call x1, Pallas kernels, head_grad(): pl.pallas_call(head_grad_kernel, out_shape=jax.ShapeDtypeStruct((depth, c...  9.61 us
    ppermute x3, waiting for transfers between devices, swap_cores(): return lax.ppermute(x, 'core', [(0, 1), (1, 0)])  8.21 us
    ppermute x3, starting transfers between devices, swap_cores(): return lax.ppermute(x, 'core', [(0, 1), (1, 0)])  5.05 us
    all_to_all x1, starting transfers between devices, exchange(): lax.all_to_all(x, AXES, split_axis=0, concat_axis=0, axis_index_groups=gr...  4.3 us
    pallas_call x1, Pallas kernels, hidden_grad(): pl.pallas_call(functools.partial(hidden_grad_kernel, block), out_shape=(j...  3.69 us
    pallas_call x1, Pallas kernels, local_logits(): pl.pallas_call(functools.partial(logits_kernel, block, 2 * columns), out_...  3.33 us
  transfers between devices with their start and end apart: 4, of which 4 were waited for; matrix products, arithmetic and copies ran while one was open for 0% of the time, Pallas kernels for 8%

profile of v2, /device:TPU:1, one launch (start us, length us, event | category | flops | bytes accessed | tf_op | source)
XLA Modules:
  0.0 113.8 jit_solution(12152028478016764843)
XLA Ops:
  0.6 0.7 broadcast_select_fusion
  1.3 0.8 select_reduce_fusion
  2.1 0.8 select_reduce_fusion.2
  3.1 1.1 pack.1
  4.2 21.5 %all_to_all.25 = bf16[8,2,19456]{2,1,0:T(2,128)(2,1)S(1)} all-to-all(bf16[8,2,19456]{2,1,0:T(2,128)(2,1)S(1)} %pack.1), channel_id=1, replica_groups={{0,1,4,5,8,9,12,13},{3,2,7,6,11,10,15,14},{68,69,64,65,76,77,72,73},{71..., dimensions={0} | all-to-all | bytes 1245184 | tf_op jit(solution)/shard_map/all_to_all | solution.py:49
  25.8 0.2 reshape.37
  26.7 19.4 %all_to_all.26 = bf16[8,16,8704]{2,1,0:T(8,128)(2,1)S(1)} all-to-all(bf16[8,16,8704]{2,1,0:T(8,128)(2,1)S(1)} %pad_maximum_fusion), channel_id=1, replica_groups={{0,3,68,71,24,27,92,95},{1,2,69,70,25,26,93,94},{4,7,64,67,28,31,88,91}..., dimensions={0} | all-to-all | bytes 4456448 | tf_op jit(solution)/shard_map/all_to_all | solution.py:49
  46.1 2.7 %collective-permute-start = (bf16[128,8704]{1,0:T(8,128)(2,1)S(1)}, bf16[128,8704]{1,0:T(8,128)(2,1)S(1)}, u32[]{:S(2)}, u32[]{:S(2)}) collective-permute-start(bf16[128,8704]{1,0:T(8,128)(2,1)S(1)} %bitcast.11), channel_id=1, source_target_pairs={{0,32},{32,0},{1,33},{33,1},{2,34},{34,2},{3,35},{35,3},{4,36},{36... | collective-permute-start | bytes 6684680 | tf_op jit(solution)/shard_map/ppermute | solution.py:55
  48.8 4.0 %collective-permute-done.other_ref = bf16[128,8704]{1,0:T(8,128)(2,1)S(1)} collective-permute-done((bf16[128,8704]{1,0:T(8,128)(2,1)S(1)}, bf16[128,8704]{1,0:T(8,128)(2,1)S(1)}, u32[]{:S(2)}, u32[]{:S(2)}) %collective-permute-start) | collective-permute-done | bytes 2228256 | tf_op jit(solution)/shard_map/ppermute | solution.py:55
  52.8 3.3 %logits.1 = (f32[256,768]{1,0:T(8,128)S(1)}, f32[8,128]{1,0:T(8,128)S(1)}) custom-call(bf16[128,8704]{1,0:T(8,128)(2,1)S(1)} %bitcast.12, bf16[128,8704]{1,0:T(8,128)(2,1)S(1)} %collective-permute-done.other_ref, bf16[7168,768]{1,0:T(8,128)(2,1)S(1)} %copy-done), custom_call_target="tpu_custom_call" | custom-call | flops 2818572288 | bytes 14680064 | tf_op jit(solution)/shard_map/logits/pallas_call | solution.py:119
  56.1 0.4 collective-permute-start.1
  56.5 0.8 collective-permute-done.1.theirs_ref
  57.4 13.2 %all_to_all.27.stats_ref = f32[64,8,128]{2,1,0:T(8,128)S(1)} all-to-all(f32[64,8,128]{2,1,0:T(8,128)S(1)} %merge.1), channel_id=1, replica_groups=mesh['yh'=2,'core'=2,'x'=4,'yl'=2,'z'=4] {'yh','x','yl','z'}, dimensions={0} | all-to-all | bytes 524288 | tf_op jit(solution)/shard_map/all_to_all | solution.py:260
  70.6 3.7 %hidden_grad.1 = (bf16[256,768]{1,0:T(8,128)(2,1)S(1)}, f32[128,7168]{1,0:T(8,128)S(1)}, bf16[128,7168]{1,0:T(8,128)(2,1)S(1)}) custom-call(f32[256,768]{1,0:T(8,128)S(1)} %get-tuple-element.12.logits_ref, bf16[128,8704]{1,0:T(8,128)(2,1)S(1)} %bitcast.13, bf16[128,8704]{1,0:T(8,128)(2,1)S(1)} %collective-permute-done.other_ref, ...), custom_call_target="tpu_custom_call" | custom-call | flops 2818572288 | bytes 16515072 | tf_op jit(solution)/shard_map/hidden_grad/pallas_call | solution.py:196
  74.3 2.0 %collective-permute-start.2 = (bf16[128,7168]{1,0:T(8,128)(2,1)S(1)}, bf16[128,7168]{1,0:T(8,128)(2,1)S(1)}, u32[]{:S(2)}, u32[]{:S(2)}) collective-permute-start(bf16[128,7168]{1,0:T(8,128)(2,1)S(1)} %get-tuple-element.16), channel_id=1, source_target_pairs={{0,32},{32,0},{1,33},{33,1},{2,34},{34,2},{3,35},{35,3},{4,36},{36... | collective-permute-start | bytes 5505032 | tf_op jit(solution)/shard_map/ppermute | solution.py:55
  76.2 3.4 %collective-permute-done.2 = bf16[128,7168]{1,0:T(8,128)(2,1)S(1)} collective-permute-done((bf16[128,7168]{1,0:T(8,128)(2,1)S(1)}, bf16[128,7168]{1,0:T(8,128)(2,1)S(1)}, u32[]{:S(2)}, u32[]{:S(2)}) %collective-permute-start.2) | collective-permute-done | bytes 1835040 | tf_op jit(solution)/shard_map/ppermute | solution.py:55
  79.6 1.6 %add_convert_fusion = bf16[128,7168]{1,0:T(8,128)(2,1)} fusion(f32[128,7168]{1,0:T(8,128)S(1)} %get-tuple-element.15, bf16[128,7168]{1,0:T(8,128)(2,1)S(1)} %collective-permute-done.2), kind=kLoop, calls=%fused_computation | loop fusion | flops 2752512 | bytes 7340032 | tf_op jit(solution)/shard_map/convert_element_type | solution.py:265
  81.2 4.3 %all-to-all-start.3 = ((bf16[8,16,7168]{2,1,0:T(8,128)(2,1)}), bf16[8,16,7168]{2,1,0:T(8,128)(2,1)}, u32[]{:S(2)}, u32[]{:S(2)}) async-start(bf16[8,16,7168]{2,1,0:T(8,128)(2,1)} %bitcast.15), calls=%async_computation.3 | async-start | bytes 3670016 | tf_op jit(solution)/shard_map/all_to_all | solution.py:49
  85.6 1.6 %copy-done.2 = bf16[128,8704]{1,0:T(8,128)(2,1)S(1)} copy-done((bf16[128,8704]{1,0:T(8,128)(2,1)S(1)}, bf16[128,8704]{1,0:T(8,128)(2,1)}, u32[]{:S(2)}) %copy-start.2) | copy-done | bytes 2228248
  87.2 9.6 %head_grad.1 = bf16[7168,768]{1,0:T(8,128)(2,1)} custom-call(bf16[128,8704]{1,0:T(8,128)(2,1)S(1)} %bitcast.14, bf16[128,8704]{1,0:T(8,128)(2,1)S(1)} %copy-done.2, bf16[256,768]{1,0:T(8,128)(2,1)S(1)} %get-tuple-element.17.grad_ref), custom_call_target="tpu_custom_call" | custom-call | flops 2818572288 | bytes 14680064 | tf_op jit(solution)/shard_map/head_grad/pallas_call | solution.py:224
  96.8 2.4 %all-to-all-done.3 = bf16[8,16,7168]{2,1,0:T(8,128)(2,1)} async-done(((bf16[8,16,7168]{2,1,0:T(8,128)(2,1)}), bf16[8,16,7168]{2,1,0:T(8,128)(2,1)}, u32[]{:S(2)}, u32[]{:S(2)}) %all-to-all-start.3) | async-done | bytes 1835040 | tf_op jit(solution)/shard_map/all_to_all | solution.py:49
  99.2 1.8 %reduce_sum.54 = bf16[16,7168]{1,0:T(8,128)(2,1)S(1)} reduce(bf16[8,16,7168]{2,1,0:T(8,128)(2,1)} %all-to-all-done.3, bf16[]{:T(256)} %constant.44.clone.1), dimensions={0}, to_apply=%region_3.4 | reduce | flops 802816 | bytes 2064386 | tf_op jit(solution)/shard_map/reduce_sum | solution.py:267
  101.1 11.8 %all_to_all.28 = bf16[8,2,7168]{2,1,0:T(2,128)(2,1)S(1)} all-to-all(bf16[8,2,7168]{2,1,0:T(2,128)(2,1)S(1)} %reshape.41), channel_id=1, replica_groups={{0,1,4,5,8,9,12,13},{3,2,7,6,11,10,15,14},{68,69,64,65,76,77,72,73},{71..., dimensions={0} | all-to-all | bytes 458752 | tf_op jit(solution)/shard_map/all_to_all | solution.py:49
  112.9 0.8 reduce_sum.55
  (18 shorter events, 0.9 us)
Async XLA Ops:
  26.2 26.5 %copy-start = (bf16[7168,768]{1,0:T(8,128)(2,1)S(1)}, bf16[7168,768]{1,0:T(8,128)(2,1)}, u32[]{:S(2)}) copy-start(bf16[7168,768]{1,0:T(8,128)(2,1)} %weight_ref.3) | copy-start | bytes 33030148
  46.1 6.6 %collective-permute-start = (bf16[128,8704]{1,0:T(8,128)(2,1)S(1)}, bf16[128,8704]{1,0:T(8,128)(2,1)S(1)}, u32[]{:S(2)}, u32[]{:S(2)}) collective-permute-start(bf16[128,8704]{1,0:T(8,128)(2,1)S(1)} %bitcast.11), channel_id=1, source_target_pairs={{0,32},{32,0},{1,33},{33,1},{2,34},{34,2},{3,35},{35,3},{4,36},{36... | collective-permute-start | bytes 6684680 | tf_op jit(solution)/shard_map/ppermute | solution.py:55
  52.8 17.8 %copy-start.1 = (bf16[128,8704]{1,0:T(8,128)(2,1)}, bf16[128,8704]{1,0:T(8,128)(2,1)S(1)}, u32[]{:S(2)}) copy-start(bf16[128,8704]{1,0:T(8,128)(2,1)S(1)} %collective-permute-done.other_ref) | copy-start | bytes 6684676
  56.1 1.3 %collective-permute-start.1 = (f32[8,128]{1,0:T(8,128)S(1)}, f32[8,128]{1,0:T(8,128)S(1)}, u32[]{:S(2)}, u32[]{:S(2)}) collective-permute-start(f32[8,128]{1,0:T(8,128)S(1)} %get-tuple-element.13.mine_ref), channel_id=1, source_target_pairs={{0,32},{32,0},{1,33},{33,1},{2,34},{34,2},{3,35},{35,3},{4,36},{36... | collective-permute-start | bytes 12296 | tf_op jit(solution)/shard_map/ppermute | solution.py:55
  74.3 5.4 %collective-permute-start.2 = (bf16[128,7168]{1,0:T(8,128)(2,1)S(1)}, bf16[128,7168]{1,0:T(8,128)(2,1)S(1)}, u32[]{:S(2)}, u32[]{:S(2)}) collective-permute-start(bf16[128,7168]{1,0:T(8,128)(2,1)S(1)} %get-tuple-element.16), channel_id=1, source_target_pairs={{0,32},{32,0},{1,33},{33,1},{2,34},{34,2},{3,35},{35,3},{4,36},{36... | collective-permute-start | bytes 5505032 | tf_op jit(solution)/shard_map/ppermute | solution.py:55
  81.2 18.0 %all-to-all-start.3 = ((bf16[8,16,7168]{2,1,0:T(8,128)(2,1)}), bf16[8,16,7168]{2,1,0:T(8,128)(2,1)}, u32[]{:S(2)}, u32[]{:S(2)}) async-start(bf16[8,16,7168]{2,1,0:T(8,128)(2,1)} %bitcast.15), calls=%async_computation.3 | async-start | bytes 3670016 | tf_op jit(solution)/shard_map/all_to_all | solution.py:49
  85.5 1.6 %copy-start.2 = (bf16[128,8704]{1,0:T(8,128)(2,1)S(1)}, bf16[128,8704]{1,0:T(8,128)(2,1)}, u32[]{:S(2)}) copy-start(bf16[128,8704]{1,0:T(8,128)(2,1)} %copy-done.1) | copy-start | bytes 6684676

commit v3 on v2

v3 whole, which is shorter than its diff:
```python
import functools

import jax
import jax.numpy as jnp
import numpy as np
from jax import lax
from jax.experimental import pallas as pl
from jax.experimental.pallas import tpu as pltpu
from jax.sharding import Mesh
from jax.sharding import PartitionSpec as P

grad_scale = 256.0

AXES = ("yh", "core", "x", "yl", "z")
CHIPS = ("yh", "x", "yl", "z")
SIZES = (2, 2, 4, 2, 4)
PEERS = 8
ROWS = 2
HALF = 128
MIB = 1 << 20


def device_at(x, y, z, core):
    return int(np.ravel_multi_index((y // 2, core, x, y % 2, z), SIZES))


PLACE = {(0, 0): 0, (1, 0): 1, (1, 1): 2, (0, 1): 3}


def chip(e, f):
    return tuple(PLACE[(e >> k) & 1, (f >> k) & 1] for k in (2, 1, 0))


def device(core, first, second, to=None):
    place = chip(first, second) if core == 0 else chip(second, first)
    return device_at(*place, core if to is None else to)


FIRST = [[device(c, v, s) for v in range(8)] for c in (0, 1) for s in range(8)]
SECOND = [[device(c, s, v) for v in range(8)] for c in (0, 1) for s in range(8)]
ORDER = [
    [ROWS * device(c, first, second) + r for second in range(8) for first in range(8) for r in range(ROWS)]
    for c in (0, 1)
]

def exchange(x, groups):
    return lax.all_to_all(
        x, AXES, split_axis=0, concat_axis=0, axis_index_groups=groups, tiled=True
    )


def swap_cores(x):
    return lax.ppermute(x, "core", [(0, 1), (1, 0)])


def pack_kernel(columns, hidden_ref, ref_ref, out_ref):
    core = lax.axis_index("core")
    for mine in (0, 1):

        @pl.when(core == mine)
        def _(mine=mine):
            for first in range(PEERS):
                target = 0
                for second in range(PEERS):
                    for to in (mine, 1 - mine):
                        source = device(mine, first, second, to) * columns
                        out_ref[first, :, target : target + columns] = ref_ref[:, source : source + columns]
                        target += columns

    rows = hidden_ref[...]
    for peer in range(PEERS):
        out_ref[peer, :, 2 * PEERS * columns :] = rows


def pack(hidden, ref_logprobs, columns):
    width = 2 * PEERS * columns + hidden.shape[1]
    whole = lambda shape: pl.BlockSpec(shape, lambda i: (0,) * len(shape))
    return pl.pallas_call(
        functools.partial(pack_kernel, columns),
        out_shape=jax.ShapeDtypeStruct((PEERS, ROWS, width), hidden.dtype),
        grid=(1,),
        in_specs=[whole(hidden.shape), whole(ref_logprobs.shape)],
        out_specs=whole((PEERS, ROWS, width)),
        compiler_params=pltpu.CompilerParams(vmem_limit_bytes=8 * MIB),
        name="pack",
    )(pltpu.with_memory_space_constraint(hidden, pltpu.HBM), pltpu.with_memory_space_constraint(ref_logprobs, pltpu.HBM))


def spread_kernel(columns, in_ref, rows_ref, lp_ref):
    depth = rows_ref.shape[1]
    first = in_ref.shape[2] - depth

    def rows(start, size):
        parts = [in_ref[peer, :, start : start + size].astype(jnp.float32) for peer in range(PEERS)]
        return jnp.concatenate(parts, axis=0).astype(rows_ref.dtype)

    block = 512
    for start in range(0, depth, block):
        rows_ref[:, start : start + block] = rows(first + start, block)
    for peer in range(PEERS):
        lp_ref[peer] = rows(peer * 2 * columns, 2 * columns)


def spread(got, depth, columns):
    vmem = pl.BlockSpec(memory_space=pltpu.VMEM)
    rows, lp = pl.pallas_call(
        functools.partial(spread_kernel, columns),
        out_shape=(
            jax.ShapeDtypeStruct((PEERS * ROWS, depth), got.dtype),
            jax.ShapeDtypeStruct((PEERS, PEERS * ROWS, 2 * columns), got.dtype),
        ),
        in_specs=[vmem],
        out_specs=(vmem, vmem),
        compiler_params=pltpu.CompilerParams(vmem_limit_bytes=8 * MIB),
        name="spread",
    )(got)
    rows = jnp.broadcast_to(rows[None], (PEERS,) + rows.shape)
    return jnp.concatenate([rows, lp], axis=2)


def token_order(core):
    place = lax.broadcasted_iota(jnp.int32, (1, HALF), 1)
    second, first, row = place >> 4, (place >> 1) & 7, place & 1
    e = jnp.where(core == 0, first, second)
    f = first + second - e
    low = e ^ f
    bit = lambda v, k: (v >> k) & 1
    index = bit(f, 1) * 2 + core
    index = index * 4 + 2 * bit(f, 2) + bit(low, 2)
    index = index * 2 + bit(low, 1)
    index = index * 4 + 2 * bit(f, 0) + bit(low, 0)
    return ROWS * index + row


def token_lines(columns, id_ref, mask_ref, advantage_ref):
    core = lax.axis_index("core")
    mine = lax.axis_index(AXES)
    other = mine + (1 - 2 * core) * (SIZES[2] * SIZES[3] * SIZES[4])
    tokens = id_ref.shape[1]
    lines = [
        id_ref[...].astype(jnp.float32),
        grad_scale * mask_ref[...].astype(jnp.float32),
        advantage_ref[...],
        jnp.zeros((HALF - 3, tokens), jnp.float32),
    ]
    table = jnp.concatenate(lines, axis=0).T
    here = lax.broadcasted_iota(jnp.int32, (tokens, HALF), 0) == token_order(core)
    ids, weighting, advantage = (
        jnp.sum(jnp.where(here, table[:, i : i + 1], 0.0), axis=0, keepdims=True) for i in range(3)
    )
    places = [ids - (d * columns).astype(jnp.float32) for d in (mine, other)]
    return jnp.concatenate(places + [weighting, advantage, jnp.zeros((4, HALF), jnp.float32)], axis=0)


def logits_kernel(
    block, own_ref, weight_ref, other_weight_ref, id_ref, mask_ref, advantage_ref, logits_ref, stats_ref, token_ref
):
    depth, columns = weight_ref.shape
    for side, w_ref in enumerate((weight_ref, other_weight_ref)):
        here = slice(side * columns, (side + 1) * columns)
        for step in range(depth // block):
            rows = slice(step * block, (step + 1) * block)
            part = jnp.dot(own_ref[:, rows], w_ref[rows, :], preferred_element_type=jnp.float32)
            if step == 0:
                logits_ref[:, here] = part
            else:
                logits_ref[:, here] += part
    token_ref[...] = token_lines(columns, id_ref, mask_ref, advantage_ref)
    logits = logits_ref[...]
    top = jnp.max(logits, axis=1, keepdims=True)
    shifted = logits - top
    scaled = jnp.exp(shifted)
    total = jnp.sum(scaled, axis=1, keepdims=True)
    cross = jnp.sum(scaled * (shifted - own_ref[:, depth:].astype(jnp.float32)), axis=1, keepdims=True)
    lane = lax.broadcasted_iota(jnp.int32, (HALF, HALF), 1)
    tile = jnp.where(lane == 0, top, jnp.where(lane == 1, total, cross)).T[:8]
    stats_ref[...] = jnp.broadcast_to(tile[None], stats_ref.shape)


def local_logits(own, weight, other_weight, tokens, peers, block=1024):
    depth, columns = weight.shape
    vmem = pl.BlockSpec(memory_space=pltpu.VMEM)
    return pl.pallas_call(
        functools.partial(logits_kernel, block),
        out_shape=(
            jax.ShapeDtypeStruct((HALF, 2 * columns), jnp.float32),
            jax.ShapeDtypeStruct((peers, 8, HALF), jnp.float32),
            jax.ShapeDtypeStruct((8, HALF), jnp.float32),
        ),
        in_specs=[vmem] * 6,
        out_specs=(vmem,) * 3,
        compiler_params=pltpu.CompilerParams(vmem_limit_bytes=16 * MIB),
        cost_estimate=pl.CostEstimate(
            flops=4 * HALF * depth * columns, bytes_accessed=4 * depth * columns, transcendentals=0
        ),
        name="logits",
    )(own, weight, other_weight, *(v.reshape(1, -1) for v in tokens))


def hidden_grad_kernel(
    block, logits_ref, own_ref, stats_ref, token_ref, weight_ref, other_weight_ref,
    grad_ref, other_grad_ref, out_ref, sums, sems,
):
    depth, columns = weight_ref.shape
    tops, totals, crosses = (stats_ref[:, i, :] for i in range(3))
    top = jnp.max(tops, axis=0, keepdims=True)
    below = tops - top
    factor = jnp.exp(below)
    total = jnp.sum(factor * totals, axis=0, keepdims=True)
    cross = jnp.sum(factor * (crosses + below * totals), axis=0, keepdims=True)
    log_total = jnp.log(total)
    divergence = cross / total - log_total
    lines = [top, log_total, divergence, token_ref[0:4, :], jnp.zeros((HALF - 7, HALF), jnp.float32)]
    table = jnp.concatenate(lines, axis=0).T
    row_top, row_log, row_div, place, other_place, weighting, advantage = (table[:, i : i + 1] for i in range(7))
    for side, (g_ref, chosen) in enumerate(((grad_ref, place), (other_grad_ref, other_place))):
        here = slice(side * columns, (side + 1) * columns)
        log_probs = (logits_ref[:, here] - row_top) - row_log
        chance = jnp.exp(log_probs)
        entry = lax.broadcasted_iota(jnp.int32, log_probs.shape, 1).astype(jnp.float32)
        picked = jnp.where(entry == chosen, 1.0, 0.0)
        lp = own_ref[:, depth + side * columns : depth + (side + 1) * columns].astype(jnp.float32)
        grad = weighting * (chance * (log_probs - lp - row_div) - advantage * (picked - chance))
        g_ref[...] = grad.astype(g_ref.dtype)

    def copy(step):
        here = pl.ds(step * block, block)
        return pltpu.make_async_copy(sums.at[:, here], out_ref.at[:, here], sems.at[step])

    for step in range(depth // block):
        here = slice(step * block, (step + 1) * block)
        total = [
            lax.dot_general(w_ref[here, :], g_ref[...], (((1,), (1,)), ((), ())), preferred_element_type=jnp.float32)
            for g_ref, w_ref in ((grad_ref, weight_ref), (other_grad_ref, other_weight_ref))
        ]
        sums[:, here] = (total[0] + total[1]).T.astype(sums.dtype)
        copy(step).start()
    for step in range(depth // block):
        copy(step).wait()


def hidden_grad(logits, own, stats, token, weight, other_weight, block=1024):
    depth, columns = weight.shape
    part = jax.ShapeDtypeStruct((HALF, columns), weight.dtype)
    return pl.pallas_call(
        functools.partial(hidden_grad_kernel, block),
        out_shape=(part, part, pltpu.HBM((HALF, depth), weight.dtype)),
        in_specs=[pl.BlockSpec(memory_space=pltpu.VMEM)] * 6,
        out_specs=(
            pl.BlockSpec(memory_space=pltpu.VMEM),
            pl.BlockSpec(memory_space=pltpu.VMEM),
            pl.BlockSpec(memory_space=pltpu.HBM),
        ),
        scratch_shapes=[pltpu.VMEM((HALF, depth), weight.dtype), pltpu.SemaphoreType.DMA((depth // block,))],
        compiler_params=pltpu.CompilerParams(vmem_limit_bytes=16 * MIB),
        cost_estimate=pl.CostEstimate(
            flops=8 * HALF * depth * columns, bytes_accessed=4 * depth * columns, transcendentals=0
        ),
        name="hidden_grad",
    )(logits, own, stats, token, weight, other_weight)


def sum_kernel(part_ref, out_ref, block=1024):
    depth = part_ref.shape[2]
    for start in range(0, depth, block):
        here = slice(start, start + block)
        parts = [part_ref[peer, :, here].astype(jnp.float32) for peer in range(PEERS)]
        while len(parts) > 1:
            parts = [a + b for a, b in zip(parts[::2], parts[1::2])]
        out_ref[:, here] = parts[0].astype(out_ref.dtype)


def add_up(parts):
    return pl.pallas_call(
        sum_kernel,
        out_shape=jax.ShapeDtypeStruct(parts.shape[1:], parts.dtype),
        in_specs=[pl.BlockSpec(memory_space=pltpu.VMEM)],
        out_specs=pl.BlockSpec(memory_space=pltpu.VMEM),
        compiler_params=pltpu.CompilerParams(vmem_limit_bytes=8 * MIB),
        name="add_up",
    )(pltpu.with_memory_space_constraint(parts, pltpu.VMEM))


def head_grad_kernel(own_ref, other_ref, own_grad_ref, other_grad_ref, out_ref):
    x = jnp.concatenate([own_ref[...], other_ref[...]], axis=0)
    grad = jnp.concatenate([own_grad_ref[...], other_grad_ref[...]], axis=0)
    out_ref[...] = lax.dot_general(
        x, grad, (((0,), (0,)), ((), ())), preferred_element_type=jnp.float32
    ).astype(out_ref.dtype)


def head_grad(own, other, own_grad, other_grad, depth, block=1792):
    tokens, columns = own_grad.shape
    x_spec = pl.BlockSpec((HALF, block), lambda k: (0, k))
    grad_spec = pl.BlockSpec(own_grad.shape, lambda k: (0, 0))
    return pl.pallas_call(
        head_grad_kernel,
        out_shape=jax.ShapeDtypeStruct((depth, columns), own_grad.dtype),
        grid=(depth // block,),
        in_specs=[x_spec, x_spec, grad_spec, grad_spec],
        out_specs=pl.BlockSpec((block, columns), lambda k: (k, 0)),
        compiler_params=pltpu.CompilerParams(vmem_limit_bytes=16 * MIB),
        cost_estimate=pl.CostEstimate(
            flops=4 * tokens * depth * columns, bytes_accessed=2 * depth * (columns + 2 * tokens), transcendentals=0
        ),
        name="head_grad",
    )(own, other, own_grad, other_grad)


def local(hidden, head_weight, ref_logprobs, token_ids, response_mask, advantages):
    depth, columns = head_weight.shape
    other_weight = pltpu.with_memory_space_constraint(swap_cores(head_weight), pltpu.VMEM)
    weight = pltpu.with_memory_space_constraint(head_weight, pltpu.VMEM)

    sent = pack(hidden, ref_logprobs, columns)
    sent = spread(exchange(sent, FIRST), depth, columns)
    own = exchange(sent, SECOND).reshape(HALF, depth + 2 * columns)
    other = swap_cores(own)

    tokens = (token_ids, response_mask, advantages)
    near = pltpu.with_memory_space_constraint(own, pltpu.VMEM)
    logits, stats, token = local_logits(near, weight, other_weight, tokens, 64)
    stats = lax.all_to_all(stats, CHIPS, split_axis=0, concat_axis=0, tiled=True)

    grad, theirs, part = hidden_grad(logits, near, stats, token, weight, other_weight)
    grad_head = head_grad(own, other, grad, swap_cores(theirs), depth)

    part = exchange(part.reshape(PEERS, PEERS * ROWS, depth), SECOND)
    part = add_up(part)
    part, grad_head = lax.optimization_barrier((part.reshape(PEERS, ROWS, depth), grad_head))
    grad_hidden = add_up(exchange(part, FIRST))
    return grad_hidden, grad_head


def solution(mesh):
    fine = Mesh(mesh.devices.reshape(SIZES), AXES)
    return jax.shard_map(
        local,
        mesh=fine,
        in_specs=(P(AXES, None), P(None, AXES), P(AXES, None), P(), P(), P()),
        out_specs=(P(AXES, None), P(None, AXES)),
        check_vma=False,
    )
```

time: 114 us -> 106 us (0.930)
  other arithmetic: 6.79 us -> 0.17 us
  waiting for transfers between devices: 10.6 us -> 4.65 us
  Pallas kernels: 17.7 us -> 22 us
  local copies, waits for them, and re-layouts: 2.49 us -> 0.96 us
  blocking collectives: 66 us -> 67.3 us
    ppermute x3, waiting for transfers between devices: 8.21 us -> 1.07 us  [swap_cores(): return lax.ppermute(x, 'core', [(0, 1), (1, 0)])]
    pallas_call x3 -> x5, Pallas kernels: 7.05 us -> 13.5 us  [the longest x1 7.33 us: hidden_grad(): pl.pallas_call(functools.partial(hidden_grad_kernel, block), out_shape=(p...]
    reduce_sum x4 -> x0, other arithmetic: 4.27 us -> none  [the longest x1 1.82 us: local(): part = jnp.sum(part.astype(jnp.float32), axis=0).astype(hidden.dtype)]
    pallas_call x1, Pallas kernels: 9.61 us -> 7.41 us  [head_grad(): pl.pallas_call(head_grad_kernel, out_shape=jax.ShapeDtypeStruct((depth, c...]
    convert_element_type x2 -> x0, other arithmetic: 1.59 us -> none  [the longest x1 1.59 us: local(): part = (mine + swap_cores(theirs).astype(jnp.float32)).astype(hidden.dtype)]
    all_to_all x1, waiting for transfers between devices: 2.42 us -> 3.58 us  [exchange(): lax.all_to_all(x, AXES, split_axis=0, concat_axis=0, axis_index_groups=gr...]
  transfers between devices with their start and end apart: 4 -> 4, of which waited for: 4 -> 2; matrix products, arithmetic and copies ran while one was open for 0% -> 0% of each run, Pallas kernels for 8% -> 19%
where the time goes in v3:
time: 106 us; the launch traced here: 105 us
  blocking collectives  67.3 us (63%)
  Pallas kernels  22 us (21%)
  starting transfers between devices  9.53 us (9%)
  waiting for transfers between devices  4.65 us (4%)
    all_to_all x3, blocking collectives, exchange(): lax.all_to_all(x, AXES, split_axis=0, concat_axis=0, axis_index_groups=gr...  53.7 us
    all_to_all x1, blocking collectives, local(): lax.all_to_all(stats, CHIPS, split_axis=0, concat_axis=0, tiled=True)  13.6 us
    pallas_call x1, Pallas kernels, head_grad(): pl.pallas_call(head_grad_kernel, out_shape=jax.ShapeDtypeStruct((depth, c...  7.41 us
    pallas_call x1, Pallas kernels, hidden_grad(): pl.pallas_call(functools.partial(hidden_grad_kernel, block), out_shape=(p...  7.33 us
    ppermute x3, starting transfers between devices, swap_cores(): return lax.ppermute(x, 'core', [(0, 1), (1, 0)])  5.09 us
    all_to_all x1, starting transfers between devices, exchange(): lax.all_to_all(x, AXES, split_axis=0, concat_axis=0, axis_index_groups=gr...  4.44 us
    all_to_all x1, waiting for transfers between devices, exchange(): lax.all_to_all(x, AXES, split_axis=0, concat_axis=0, axis_index_groups=gr...  3.58 us
    pallas_call x1, Pallas kernels, local_logits(): pl.pallas_call(functools.partial(logits_kernel, block), out_shape=(jax.Sh...  3.39 us
  transfers between devices with their start and end apart: 4, of which 2 were waited for; matrix products, arithmetic and copies ran while one was open for 0% of the time, Pallas kernels for 19%

profile of v3, /device:TPU:1, one launch (start us, length us, event | category | flops | bytes accessed | tf_op | source)
XLA Modules:
  0.0 105.3 jit_solution(12908920308092793107)
XLA Ops:
  0.6 1.5 %collective-permute-start = (bf16[7168,768]{1,0:T(8,128)(2,1)}, bf16[7168,768]{1,0:T(8,128)(2,1)S(1)}, u32[]{:S(2)}, u32[]{:S(2)}) collective-permute-start(bf16[7168,768]{1,0:T(8,128)(2,1)} %weight_ref.3), channel_id=1, source_target_pairs={{0,32},{32,0},{1,33},{33,1},{2,34},{34,2},{3,35},{35,3},{4,36},{36... | collective-permute-start | bytes 33030152 | tf_op jit(solution)/shard_map/ppermute | solution.py:53
  2.1 1.1 %pack.1 = bf16[8,2,19456]{2,1,0:T(2,128)(2,1)S(1)} custom-call(bf16[2,7168]{1,0:T(2,128)(2,1)} %hidden_ref.1, bf16[2,98304]{1,0:T(2,128)(2,1)} %ref_ref.1), custom_call_target="tpu_custom_call" | custom-call | tf_op jit(solution)/shard_map/pack/pallas_call | solution.py:78
  3.2 20.8 %all_to_all.25.in_ref = bf16[8,2,19456]{2,1,0:T(2,128)(2,1)S(1)} all-to-all(bf16[8,2,19456]{2,1,0:T(2,128)(2,1)S(1)} %pack.1), channel_id=1, replica_groups={{0,1,4,5,8,9,12,13},{3,2,7,6,11,10,15,14},{68,69,64,65,76,77,72,73},{71..., dimensions={0} | all-to-all | bytes 1245184 | tf_op jit(solution)/shard_map/all_to_all | solution.py:47
  24.0 0.4 spread.1
  24.4 0.2 broadcast_in_dim.2
  24.6 0.2 pad_maximum_fusion
  24.8 0.0 copy-start.1
  24.8 0.0 copy-start.2
  24.8 19.4 %all_to_all.26 = bf16[8,16,8704]{2,1,0:T(8,128)(2,1)S(1)} all-to-all(bf16[8,16,8704]{2,1,0:T(8,128)(2,1)S(1)} %pad_maximum_fusion), channel_id=1, replica_groups={{0,3,68,71,24,27,92,95},{1,2,69,70,25,26,93,94},{4,7,64,67,28,31,88,91}..., dimensions={0} | all-to-all | bytes 4456448 | tf_op jit(solution)/shard_map/all_to_all | solution.py:47
  44.2 2.0 %collective-permute-start.1 = (bf16[128,8704]{1,0:T(8,128)(2,1)S(1)}, bf16[128,8704]{1,0:T(8,128)(2,1)}, u32[]{:S(2)}, u32[]{:S(2)}) collective-permute-start(bf16[128,8704]{1,0:T(8,128)(2,1)S(1)} %bitcast.5), channel_id=1, source_target_pairs={{0,32},{32,0},{1,33},{33,1},{2,34},{34,2},{3,35},{35,3},{4,36},{36... | collective-permute-start | bytes 6684680 | tf_op jit(solution)/shard_map/ppermute | solution.py:53
  46.3 3.4 %logits.1 = (f32[128,1536]{1,0:T(8,128)S(1)}, f32[64,8,128]{2,1,0:T(8,128)S(1)}, f32[8,128]{1,0:T(8,128)S(1)}) custom-call(bf16[128,8704]{1,0:T(8,128)(2,1)S(1)} %bitcast.6, bf16[7168,768]{1,0:T(8,128)(2,1)S(1)} %copy-done, bf16[7168,768]{1,0:T(8,128)(2,1)S(1)} %collective-permute-done.other_weight_ref, s32[1,256]{1,0:T(1,128)S(1)} %bitcast.9, ...), custom_call_target="tpu_custom_call" | custom-call | flops 2818572288 | bytes 22020096 | tf_op jit(solution)/shard_map/logits/pallas_call | solution.py:183
  49.7 13.6 %all_to_all.27.stats_ref = f32[64,8,128]{2,1,0:T(8,128)S(1)} all-to-all(f32[64,8,128]{2,1,0:T(8,128)S(1)} %get-tuple-element.15), channel_id=1, replica_groups=mesh['yh'=2,'core'=2,'x'=4,'yl'=2,'z'=4] {'yh','x','yl','z'}, dimensions={0} | all-to-all | bytes 524288 | tf_op jit(solution)/shard_map/all_to_all | solution.py:323
  63.2 7.3 %hidden_grad.1 = (bf16[128,768]{1,0:T(8,128)(2,1)S(1)}, bf16[128,768]{1,0:T(8,128)(2,1)S(1)}, bf16[128,7168]{1,0:T(8,128)(2,1)}) custom-call(f32[128,1536]{1,0:T(8,128)S(1)} %get-tuple-element.14.logits_ref, bf16[128,8704]{1,0:T(8,128)(2,1)S(1)} %bitcast.7, f32[64,8,128]{2,1,0:T(8,128)S(1)} %all_to_all.27.stats_ref, ...), custom_call_target="tpu_custom_call" | custom-call | flops 5637144576 | bytes 22020096 | tf_op jit(solution)/shard_map/hidden_grad/pallas_call | solution.py:245
  70.6 0.0 copy-start.4
  70.6 0.7 copy-done.4
  71.2 4.4 %all-to-all-start.3 = ((bf16[8,16,7168]{2,1,0:T(8,128)(2,1)}), bf16[8,16,7168]{2,1,0:T(8,128)(2,1)}, u32[]{:S(2)}, u32[]{:S(2)}) async-start(bf16[8,16,7168]{2,1,0:T(8,128)(2,1)} %bitcast.12), calls=%async_computation.3 | async-start | bytes 3670016 | tf_op jit(solution)/shard_map/all_to_all | solution.py:47
  75.7 1.6 %collective-permute-start.2 = (bf16[128,768]{1,0:T(8,128)(2,1)S(1)}, bf16[128,768]{1,0:T(8,128)(2,1)S(1)}, u32[]{:S(2)}, u32[]{:S(2)}) collective-permute-start(bf16[128,768]{1,0:T(8,128)(2,1)S(1)} %copy-done.5), channel_id=1, source_target_pairs={{0,32},{32,0},{1,33},{33,1},{2,34},{34,2},{3,35},{35,3},{4,36},{36... | collective-permute-start | bytes 589832 | tf_op jit(solution)/shard_map/ppermute | solution.py:53
  77.3 1.1 %collective-permute-done.2.other_grad_ref = bf16[128,768]{1,0:T(8,128)(2,1)S(1)} collective-permute-done((bf16[128,768]{1,0:T(8,128)(2,1)S(1)}, bf16[128,768]{1,0:T(8,128)(2,1)S(1)}, u32[]{:S(2)}, u32[]{:S(2)}) %collective-permute-start.2) | collective-permute-done | bytes 196640 | tf_op jit(solution)/shard_map/ppermute | solution.py:53
  78.4 7.4 %head_grad.1 = bf16[7168,768]{1,0:T(8,128)(2,1)} custom-call(bf16[128,8704]{1,0:T(8,128)(2,1)S(1)} %bitcast.8, bf16[128,8704]{1,0:T(8,128)(2,1)} %collective-permute-done.1.other_ref, bf16[128,768]{1,0:T(8,128)(2,1)S(1)} %get-tuple-element.18.own_grad_ref, bf16[128,768]{1,0:T(8,128)(2,1)S(1)} %collective-permute-done.2.other_grad_ref), custom_call_target="tpu_custom_call" | custom-call | flops 2818572288 | bytes 14680064 | tf_op jit(solution)/shard_map/head_grad/pallas_call | solution.py:296
  85.8 3.6 %all-to-all-done.3.part_ref = bf16[8,16,7168]{2,1,0:T(8,128)(2,1)} async-done(((bf16[8,16,7168]{2,1,0:T(8,128)(2,1)}), bf16[8,16,7168]{2,1,0:T(8,128)(2,1)}, u32[]{:S(2)}, u32[]{:S(2)}) %all-to-all-start.3) | async-done | bytes 1835040 | tf_op jit(solution)/shard_map/all_to_all | solution.py:47
  89.4 1.7 %add_up.2 = bf16[16,7168]{1,0:T(8,128)(2,1)S(1)} custom-call(bf16[8,16,7168]{2,1,0:T(8,128)(2,1)} %all-to-all-done.3.part_ref), custom_call_target="tpu_custom_call" | custom-call | tf_op jit(solution)/shard_map/add_up/pallas_call | solution.py:274
  91.1 0.1 reshape.28
  91.2 13.5 %all_to_all.28.part_ref = bf16[8,2,7168]{2,1,0:T(2,128)(2,1)S(1)} all-to-all(bf16[8,2,7168]{2,1,0:T(2,128)(2,1)S(1)} %reshape.28), channel_id=1, replica_groups={{0,1,4,5,8,9,12,13},{3,2,7,6,11,10,15,14},{68,69,64,65,76,77,72,73},{71..., dimensions={0} | all-to-all | bytes 458752 | tf_op jit(solution)/shard_map/all_to_all | solution.py:47
  104.7 0.7 add_up.3
  (10 shorter events, 0.0 us)
Async XLA Ops:
  0.6 45.6 %collective-permute-start = (bf16[7168,768]{1,0:T(8,128)(2,1)}, bf16[7168,768]{1,0:T(8,128)(2,1)S(1)}, u32[]{:S(2)}, u32[]{:S(2)}) collective-permute-start(bf16[7168,768]{1,0:T(8,128)(2,1)} %weight_ref.3), channel_id=1, source_target_pairs={{0,32},{32,0},{1,33},{33,1},{2,34},{34,2},{3,35},{35,3},{4,36},{36... | collective-permute-start | bytes 33030152 | tf_op jit(solution)/shard_map/ppermute | solution.py:53
  24.0 22.2 %copy-start = (bf16[7168,768]{1,0:T(8,128)(2,1)S(1)}, bf16[7168,768]{1,0:T(8,128)(2,1)}, u32[]{:S(2)}) copy-start(bf16[7168,768]{1,0:T(8,128)(2,1)} %weight_ref.3) | copy-start | bytes 33030148
  24.8 21.5 %copy-start.1 = (s32[256]{0:T(256)S(1)}, s32[256]{0:T(256)}, u32[]{:S(2)}) copy-start(s32[256]{0:T(256)} %param.9) | copy-start | bytes 3076
  24.8 21.5 %copy-start.2 = (s32[256]{0:T(256)S(1)}, s32[256]{0:T(256)}, u32[]{:S(2)}) copy-start(s32[256]{0:T(256)} %param.10) | copy-start | bytes 3076
  24.8 21.5 %copy-start.3 = (f32[256]{0:T(256)S(1)}, f32[256]{0:T(256)}, u32[]{:S(2)}) copy-start(f32[256]{0:T(256)} %param.11) | copy-start | bytes 3076
  44.2 33.1 %collective-permute-start.1 = (bf16[128,8704]{1,0:T(8,128)(2,1)S(1)}, bf16[128,8704]{1,0:T(8,128)(2,1)}, u32[]{:S(2)}, u32[]{:S(2)}) collective-permute-start(bf16[128,8704]{1,0:T(8,128)(2,1)S(1)} %bitcast.5), channel_id=1, source_target_pairs={{0,32},{32,0},{1,33},{33,1},{2,34},{34,2},{3,35},{35,3},{4,36},{36... | collective-permute-start | bytes 6684680 | tf_op jit(solution)/shard_map/ppermute | solution.py:53
  70.6 0.7 copy-start.4
  71.2 4.5 %copy-start.5 = (bf16[128,768]{1,0:T(8,128)(2,1)S(1)}, bf16[128,768]{1,0:T(8,128)(2,1)}, u32[]{:S(2)}) copy-start(bf16[128,768]{1,0:T(8,128)(2,1)} %copy-done.4) | copy-start | bytes 589828
  71.2 18.1 %all-to-all-start.3 = ((bf16[8,16,7168]{2,1,0:T(8,128)(2,1)}), bf16[8,16,7168]{2,1,0:T(8,128)(2,1)}, u32[]{:S(2)}, u32[]{:S(2)}) async-start(bf16[8,16,7168]{2,1,0:T(8,128)(2,1)} %bitcast.12), calls=%async_computation.3 | async-start | bytes 3670016 | tf_op jit(solution)/shard_map/all_to_all | solution.py:47
  75.7 2.7 %collective-permute-start.2 = (bf16[128,768]{1,0:T(8,128)(2,1)S(1)}, bf16[128,768]{1,0:T(8,128)(2,1)S(1)}, u32[]{:S(2)}, u32[]{:S(2)}) collective-permute-start(bf16[128,768]{1,0:T(8,128)(2,1)S(1)} %copy-done.5), channel_id=1, source_target_pairs={{0,32},{32,0},{1,33},{33,1},{2,34},{34,2},{3,35},{35,3},{4,36},{36... | collective-permute-start | bytes 589832 | tf_op jit(solution)/shard_map/ppermute | solution.py:53

commit v4 on v3

--- a/solution.py
+++ b/solution.py
@@ -199,9 +199,10 @@
 
 def hidden_grad_kernel(
     block, logits_ref, own_ref, stats_ref, token_ref, weight_ref, other_weight_ref,
-    grad_ref, other_grad_ref, out_ref, sums, sems,
+    near_ref, far_ref, out_ref, grad_ref, other_grad_ref, sums, sems,
 ):
     depth, columns = weight_ref.shape
+    steps = depth // block
     tops, totals, crosses = (stats_ref[:, i, :] for i in range(3))
     top = jnp.max(tops, axis=0, keepdims=True)
     below = tops - top
@@ -224,8 +225,14 @@
         g_ref[...] = grad.astype(g_ref.dtype)
 
     def copy(step):
+        if step >= steps:
+            pair = ((grad_ref, near_ref), (other_grad_ref, far_ref))[step - steps]
+            return pltpu.make_async_copy(*pair, sems.at[step])
         here = pl.ds(step * block, block)
         return pltpu.make_async_copy(sums.at[:, here], out_ref.at[:, here], sems.at[step])
+
+    copy(steps).start()
+    copy(steps + 1).start()
 
     for step in range(depth // block):
         here = slice(step * block, (step + 1) * block)
@@ -235,23 +242,24 @@
         ]
         sums[:, here] = (total[0] + total[1]).T.astype(sums.dtype)
         copy(step).start()
-    for step in range(depth // block):
+    for step in range(steps + 2):
         copy(step).wait()
 
 
 def hidden_grad(logits, own, stats, token, weight, other_weight, block=1024):
     depth, columns = weight.shape
-    part = jax.ShapeDtypeStruct((HALF, columns), weight.dtype)
+    part = pltpu.HBM((HALF, columns), weight.dtype)
     return pl.pallas_call(
         functools.partial(hidden_grad_kernel, block),
         out_shape=(part, part, pltpu.HBM((HALF, depth), weight.dtype)),
         in_specs=[pl.BlockSpec(memory_space=pltpu.VMEM)] * 6,
-        out_specs=(
-            pl.BlockSpec(memory_space=pltpu.VMEM),
-            pl.BlockSpec(memory_space=pltpu.VMEM),
-            pl.BlockSpec(memory_space=pltpu.HBM),
-        ),
-        scratch_shapes=[pltpu.VMEM((HALF, depth), weight.dtype), pltpu.SemaphoreType.DMA((depth // block,))],
+        out_specs=(pl.BlockSpec(memory_space=pltpu.HBM),) * 3,
+        scratch_shapes=[
+            pltpu.VMEM((HALF, columns), weight.dtype),
+            pltpu.VMEM((HALF, columns), weight.dtype),
+            pltpu.VMEM((HALF, depth), weight.dtype),
+            pltpu.SemaphoreType.DMA((depth // block + 2,)),
+        ],
         compiler_params=pltpu.CompilerParams(vmem_limit_bytes=16 * MIB),
         cost_estimate=pl.CostEstimate(
             flops=8 * HALF * depth * columns, bytes_accessed=4 * depth * columns, transcendentals=0
@@ -260,25 +268,47 @@
     )(logits, own, stats, token, weight, other_weight)
 
 
-def sum_kernel(part_ref, out_ref, block=1024):
-    depth = part_ref.shape[2]
-    for start in range(0, depth, block):
-        here = slice(start, start + block)
-        parts = [part_ref[peer, :, here].astype(jnp.float32) for peer in range(PEERS)]
-        while len(parts) > 1:
-            parts = [a + b for a, b in zip(parts[::2], parts[1::2])]
-        out_ref[:, here] = parts[0].astype(out_ref.dtype)
-
-
-def add_up(parts):
-    return pl.pallas_call(
-        sum_kernel,
+def total_of(parts):
+    parts = [p.astype(jnp.float32) for p in parts]
+    while len(parts) > 1:
+        parts = [a + b for a, b in zip(parts[::2], parts[1::2])]
+    return parts[0]
+
+
+def sum_far_kernel(block, part_ref, out_ref, here_ref, sems):
+    steps = part_ref.shape[2] // block
+
+    def load(step):
+        columns = pl.ds(step * block, block)
+        return pltpu.make_async_copy(part_ref.at[:, :, columns], here_ref.at[:, :, columns], sems.at[step])
+
+    for step in range(steps):
+        load(step).start()
+    for step in range(steps):
+        load(step).wait()
+        columns = slice(step * block, (step + 1) * block)
+        total = total_of([here_ref[peer, :, columns] for peer in range(PEERS)])
+        out_ref[:, columns] = total.astype(out_ref.dtype)
+
+
+def sum_kernel(part_ref, out_ref):
+    out_ref[...] = total_of([part_ref[peer] for peer in range(PEERS)]).astype(out_ref.dtype)
+
+
+def add_up(parts, block=None):
+    vmem = pl.BlockSpec(memory_space=pltpu.VMEM)
+    space = pltpu.HBM if block else pltpu.VMEM
+    return pl.pallas_call(
+        functools.partial(sum_far_kernel, block) if block else sum_kernel,
         out_shape=jax.ShapeDtypeStruct(parts.shape[1:], parts.dtype),
-        in_specs=[pl.BlockSpec(memory_space=pltpu.VMEM)],
-        out_specs=pl.BlockSpec(memory_space=pltpu.VMEM),
+        in_specs=[pl.BlockSpec(memory_space=space)],
+        out_specs=vmem,
+        scratch_shapes=(
+            [pltpu.VMEM(parts.shape, parts.dtype), pltpu.SemaphoreType.DMA((parts.shape[2] // block,))] if block else []
+        ),
         compiler_params=pltpu.CompilerParams(vmem_limit_bytes=8 * MIB),
         name="add_up",
-    )(pltpu.with_memory_space_constraint(parts, pltpu.VMEM))
+    )(pltpu.with_memory_space_constraint(parts, space))
 
 
 def head_grad_kernel(own_ref, other_ref, own_grad_ref, other_grad_ref, out_ref):
@@ -304,7 +334,7 @@
             flops=4 * tokens * depth * columns, bytes_accessed=2 * depth * (columns + 2 * tokens), transcendentals=0
         ),
         name="head_grad",
-    )(own, other, own_grad, other_grad)
+    )(*(pltpu.with_memory_space_constraint(x, pltpu.HBM) for x in (own, other)), own_grad, other_grad)
 
 
 def local(hidden, head_weight, ref_logprobs, token_ids, response_mask, advantages):
@@ -315,20 +345,21 @@
     sent = pack(hidden, ref_logprobs, columns)
     sent = spread(exchange(sent, FIRST), depth, columns)
     own = exchange(sent, SECOND).reshape(HALF, depth + 2 * columns)
-    other = swap_cores(own)
 
     tokens = (token_ids, response_mask, advantages)
     near = pltpu.with_memory_space_constraint(own, pltpu.VMEM)
     logits, stats, token = local_logits(near, weight, other_weight, tokens, 64)
     stats = lax.all_to_all(stats, CHIPS, split_axis=0, concat_axis=0, tiled=True)
+    late, stats = lax.optimization_barrier((own, stats))
+    other = swap_cores(late)
 
     grad, theirs, part = hidden_grad(logits, near, stats, token, weight, other_weight)
     grad_head = head_grad(own, other, grad, swap_cores(theirs), depth)
 
     part = exchange(part.reshape(PEERS, PEERS * ROWS, depth), SECOND)
-    part = add_up(part)
-    part, grad_head = lax.optimization_barrier((part.reshape(PEERS, ROWS, depth), grad_head))
-    grad_hidden = add_up(exchange(part, FIRST))
+    part, grad_head = lax.optimization_barrier((part, grad_head))
+    part = add_up(part, 1792)
+    grad_hidden = add_up(exchange(part.reshape(PEERS, ROWS, depth), FIRST))
     return grad_hidden, grad_head
 
 

time: 106 us -> 105 us (level)
  blocking collectives: 67.3 us -> 65.9 us
  transfers between devices with their start and end apart: 4 -> 4, of which waited for: 2 -> 2; matrix products, arithmetic and copies ran while one was open for 0% -> 0% of each run, Pallas kernels for 19% -> 16%
where the time goes in v4:
time: 105 us; the launch traced here: 104 us
  blocking collectives  65.9 us (63%)
  Pallas kernels  22.3 us (21%)
  starting transfers between devices  9.12 us (9%)
  waiting for transfers between devices  5.56 us (5%)
    all_to_all x3, blocking collectives, exchange(): lax.all_to_all(x, AXES, split_axis=0, concat_axis=0, axis_index_groups=gr...  52.8 us
    all_to_all x1, blocking collectives, local(): lax.all_to_all(stats, CHIPS, split_axis=0, concat_axis=0, tiled=True)  13.1 us
    pallas_call x1, Pallas kernels, head_grad(): pl.pallas_call(head_grad_kernel, out_shape=jax.ShapeDtypeStruct((depth, c...  7.99 us
    pallas_call x1, Pallas kernels, hidden_grad(): pl.pallas_call(functools.partial(hidden_grad_kernel, block), out_shape=(p...  7.31 us
    ppermute x3, starting transfers between devices, swap_cores(): return lax.ppermute(x, 'core', [(0, 1), (1, 0)])  4.65 us
    all_to_all x1, starting transfers between devices, exchange(): lax.all_to_all(x, AXES, split_axis=0, concat_axis=0, axis_index_groups=gr...  4.47 us
    all_to_all x1, waiting for transfers between devices, exchange(): lax.all_to_all(x, AXES, split_axis=0, concat_axis=0, axis_index_groups=gr...  4.12 us
    pallas_call x1, Pallas kernels, local_logits(): pl.pallas_call(functools.partial(logits_kernel, block), out_shape=(jax.Sh...  3.39 us
  transfers between devices with their start and end apart: 4, of which 2 were waited for; matrix products, arithmetic and copies ran while one was open for 0% of the time, Pallas kernels for 16%

profile of v4, /device:TPU:1, one launch (start us, length us, event | category | flops | bytes accessed | tf_op | source)
XLA Modules:
  0.0 104.1 jit_solution(13813652019570784660)
XLA Ops:
  0.6 1.5 %collective-permute-start = (bf16[7168,768]{1,0:T(8,128)(2,1)}, bf16[7168,768]{1,0:T(8,128)(2,1)S(1)}, u32[]{:S(2)}, u32[]{:S(2)}) collective-permute-start(bf16[7168,768]{1,0:T(8,128)(2,1)} %weight_ref.3), channel_id=1, source_target_pairs={{0,32},{32,0},{1,33},{33,1},{2,34},{34,2},{3,35},{35,3},{4,36},{36... | collective-permute-start | bytes 33030152 | tf_op jit(solution)/shard_map/ppermute | solution.py:53
  2.1 1.1 %pack.1 = bf16[8,2,19456]{2,1,0:T(2,128)(2,1)S(1)} custom-call(bf16[2,7168]{1,0:T(2,128)(2,1)} %hidden_ref.1, bf16[2,98304]{1,0:T(2,128)(2,1)} %ref_ref.1), custom_call_target="tpu_custom_call" | custom-call | tf_op jit(solution)/shard_map/pack/pallas_call | solution.py:78
  3.2 20.8 %all_to_all.25.in_ref = bf16[8,2,19456]{2,1,0:T(2,128)(2,1)S(1)} all-to-all(bf16[8,2,19456]{2,1,0:T(2,128)(2,1)S(1)} %pack.1), channel_id=1, replica_groups={{0,1,4,5,8,9,12,13},{3,2,7,6,11,10,15,14},{68,69,64,65,76,77,72,73},{71..., dimensions={0} | all-to-all | bytes 1245184 | tf_op jit(solution)/shard_map/all_to_all | solution.py:47
  24.0 0.4 spread.1
  24.4 0.2 broadcast_in_dim.2
  24.6 0.2 pad_maximum_fusion
  24.8 0.0 copy-start.3
  24.8 0.0 copy-start.4
  24.8 0.0 copy-start.5
  24.8 19.4 %all_to_all.26 = bf16[8,16,8704]{2,1,0:T(8,128)(2,1)S(1)} all-to-all(bf16[8,16,8704]{2,1,0:T(8,128)(2,1)S(1)} %pad_maximum_fusion), channel_id=1, replica_groups={{0,3,68,71,24,27,92,95},{1,2,69,70,25,26,93,94},{4,7,64,67,28,31,88,91}..., dimensions={0} | all-to-all | bytes 4456448 | tf_op jit(solution)/shard_map/all_to_all | solution.py:47
  44.3 3.4 %logits.1 = (f32[128,1536]{1,0:T(8,128)S(1)}, f32[64,8,128]{2,1,0:T(8,128)S(1)}, f32[8,128]{1,0:T(8,128)S(1)}) custom-call(bf16[128,8704]{1,0:T(8,128)(2,1)S(1)} %bitcast.5, bf16[7168,768]{1,0:T(8,128)(2,1)S(1)} %copy-done, bf16[7168,768]{1,0:T(8,128)(2,1)S(1)} %collective-permute-done.other_weight_ref, s32[1,256]{1,0:T(1,128)S(1)} %bitcast.9, ...), custom_call_target="tpu_custom_call" | custom-call | flops 2818572288 | bytes 22020096 | tf_op jit(solution)/shard_map/logits/pallas_call | solution.py:183
  47.7 13.1 %all_to_all.27.stats_ref = f32[64,8,128]{2,1,0:T(8,128)S(1)} all-to-all(f32[64,8,128]{2,1,0:T(8,128)S(1)} %get-tuple-element.17), channel_id=1, replica_groups=mesh['yh'=2,'core'=2,'x'=4,'yl'=2,'z'=4] {'yh','x','yl','z'}, dimensions={0} | all-to-all | bytes 524288 | tf_op jit(solution)/shard_map/all_to_all | solution.py:352
  60.7 3.1 %collective-permute-start.1 = (bf16[128,8704]{1,0:T(8,128)(2,1)S(1)}, bf16[128,8704]{1,0:T(8,128)(2,1)}, u32[]{:S(2)}, u32[]{:S(2)}) collective-permute-start(bf16[128,8704]{1,0:T(8,128)(2,1)S(1)} %bitcast.6), channel_id=1, source_target_pairs={{0,32},{32,0},{1,33},{33,1},{2,34},{34,2},{3,35},{35,3},{4,36},{36... | collective-permute-start | bytes 6684680 | tf_op jit(solution)/shard_map/ppermute | solution.py:53
  63.8 7.3 %hidden_grad.1 = (bf16[128,768]{1,0:T(8,128)(2,1)}, bf16[128,768]{1,0:T(8,128)(2,1)}, bf16[128,7168]{1,0:T(8,128)(2,1)}) custom-call(f32[128,1536]{1,0:T(8,128)S(1)} %get-tuple-element.16.logits_ref, bf16[128,8704]{1,0:T(8,128)(2,1)S(1)} %bitcast.7, f32[64,8,128]{2,1,0:T(8,128)S(1)} %all_to_all.27.stats_ref, f32[8,128]{1,0:T(8,128)S(1)} %get-tuple-element.19.token_ref, ...), custom_call_target="tpu_custom_call" | custom-call | flops 5637144576 | bytes 22020096 | tf_op jit(solution)/shard_map/hidden_grad/pallas_call | solution.py:252
  71.1 0.0 copy-start.2
  71.1 4.5 %all-to-all-start.3 = ((bf16[8,16,7168]{2,1,0:T(8,128)(2,1)}), bf16[8,16,7168]{2,1,0:T(8,128)(2,1)}, u32[]{:S(2)}, u32[]{:S(2)}) async-start(bf16[8,16,7168]{2,1,0:T(8,128)(2,1)} %bitcast.12), calls=%async_computation.3 | async-start | bytes 3670016 | tf_op jit(solution)/shard_map/all_to_all | solution.py:47
  75.6 0.1 collective-permute-start.2
  75.7 1.4 %collective-permute-done.2.other_grad_ref = bf16[128,768]{1,0:T(8,128)(2,1)S(1)} collective-permute-done((bf16[128,768]{1,0:T(8,128)(2,1)S(1)}, bf16[128,768]{1,0:T(8,128)(2,1)S(1)}, u32[]{:S(2)}, u32[]{:S(2)}) %collective-permute-start.2) | collective-permute-done | bytes 196640 | tf_op jit(solution)/shard_map/ppermute | solution.py:53
  77.2 8.0 %head_grad.1 = bf16[7168,768]{1,0:T(8,128)(2,1)} custom-call(bf16[128,8704]{1,0:T(8,128)(2,1)} %bitcast.8, bf16[128,8704]{1,0:T(8,128)(2,1)} %collective-permute-done.1.other_ref, bf16[128,768]{1,0:T(8,128)(2,1)S(1)} %copy-done.2, bf16[128,768]{1,0:T(8,128)(2,1)S(1)} %collective-permute-done.2.other_grad_ref), custom_call_target="tpu_custom_call" | custom-call | flops 2818572288 | bytes 14680064 | tf_op jit(solution)/shard_map/head_grad/pallas_call | solution.py:326
  85.2 4.1 %all-to-all-done.3.part_ref = bf16[8,16,7168]{2,1,0:T(8,128)(2,1)} async-done(((bf16[8,16,7168]{2,1,0:T(8,128)(2,1)}), bf16[8,16,7168]{2,1,0:T(8,128)(2,1)}, u32[]{:S(2)}, u32[]{:S(2)}) %all-to-all-start.3) | async-done | bytes 1835040 | tf_op jit(solution)/shard_map/all_to_all | solution.py:47
  89.3 1.5 %add_up.2 = bf16[16,7168]{1,0:T(8,128)(2,1)S(1)} custom-call(bf16[8,16,7168]{2,1,0:T(8,128)(2,1)} %all-to-all-done.3.part_ref), custom_call_target="tpu_custom_call" | custom-call | tf_op jit(solution)/shard_map/add_up/pallas_call | solution.py:301
  90.8 0.1 reshape.28
  90.9 12.6 %all_to_all.28.part_ref = bf16[8,2,7168]{2,1,0:T(2,128)(2,1)S(1)} all-to-all(bf16[8,2,7168]{2,1,0:T(2,128)(2,1)S(1)} %reshape.28), channel_id=1, replica_groups={{0,1,4,5,8,9,12,13},{3,2,7,6,11,10,15,14},{68,69,64,65,76,77,72,73},{71..., dimensions={0} | all-to-all | bytes 458752 | tf_op jit(solution)/shard_map/all_to_all | solution.py:47
  103.5 0.7 add_up.3
  (12 shorter events, 0.0 us)
Async XLA Ops:
  0.6 43.6 %collective-permute-start = (bf16[7168,768]{1,0:T(8,128)(2,1)}, bf16[7168,768]{1,0:T(8,128)(2,1)S(1)}, u32[]{:S(2)}, u32[]{:S(2)}) collective-permute-start(bf16[7168,768]{1,0:T(8,128)(2,1)} %weight_ref.3), channel_id=1, source_target_pairs={{0,32},{32,0},{1,33},{33,1},{2,34},{34,2},{3,35},{35,3},{4,36},{36... | collective-permute-start | bytes 33030152 | tf_op jit(solution)/shard_map/ppermute | solution.py:53
  24.0 20.2 %copy-start = (bf16[7168,768]{1,0:T(8,128)(2,1)S(1)}, bf16[7168,768]{1,0:T(8,128)(2,1)}, u32[]{:S(2)}) copy-start(bf16[7168,768]{1,0:T(8,128)(2,1)} %weight_ref.3) | copy-start | bytes 33030148
  24.8 19.5 %copy-start.3 = (s32[256]{0:T(256)S(1)}, s32[256]{0:T(256)}, u32[]{:S(2)}) copy-start(s32[256]{0:T(256)} %param.9) | copy-start | bytes 3076
  24.8 19.5 %copy-start.4 = (s32[256]{0:T(256)S(1)}, s32[256]{0:T(256)}, u32[]{:S(2)}) copy-start(s32[256]{0:T(256)} %param.10) | copy-start | bytes 3076
  24.8 19.5 %copy-start.5 = (f32[256]{0:T(256)S(1)}, f32[256]{0:T(256)}, u32[]{:S(2)}) copy-start(f32[256]{0:T(256)} %param.11) | copy-start | bytes 3076
  44.2 19.6 %copy-start.1 = (bf16[8,16,8704]{2,1,0:T(8,128)(2,1)}, bf16[8,16,8704]{2,1,0:T(8,128)(2,1)S(1)}, u32[]{:S(2)}) copy-start(bf16[8,16,8704]{2,1,0:T(8,128)(2,1)S(1)} %all_to_all.26) | copy-start | bytes 6684676
  60.7 16.4 %collective-permute-start.1 = (bf16[128,8704]{1,0:T(8,128)(2,1)S(1)}, bf16[128,8704]{1,0:T(8,128)(2,1)}, u32[]{:S(2)}, u32[]{:S(2)}) collective-permute-start(bf16[128,8704]{1,0:T(8,128)(2,1)S(1)} %bitcast.6), channel_id=1, source_target_pairs={{0,32},{32,0},{1,33},{33,1},{2,34},{34,2},{3,35},{35,3},{4,36},{36... | collective-permute-start | bytes 6684680 | tf_op jit(solution)/shard_map/ppermute | solution.py:53
  71.1 4.5 %copy-start.6 = (bf16[128,768]{1,0:T(8,128)(2,1)S(1)}, bf16[128,768]{1,0:T(8,128)(2,1)}, u32[]{:S(2)}) copy-start(bf16[128,768]{1,0:T(8,128)(2,1)} %get-tuple-element.23) | copy-start | bytes 589828
  71.1 6.0 %copy-start.2 = (bf16[128,768]{1,0:T(8,128)(2,1)S(1)}, bf16[128,768]{1,0:T(8,128)(2,1)}, u32[]{:S(2)}) copy-start(bf16[128,768]{1,0:T(8,128)(2,1)} %get-tuple-element.22.own_grad_ref) | copy-start | bytes 589828
  71.1 18.1 %all-to-all-start.3 = ((bf16[8,16,7168]{2,1,0:T(8,128)(2,1)}), bf16[8,16,7168]{2,1,0:T(8,128)(2,1)}, u32[]{:S(2)}, u32[]{:S(2)}) async-start(bf16[8,16,7168]{2,1,0:T(8,128)(2,1)} %bitcast.12), calls=%async_computation.3 | async-start | bytes 3670016 | tf_op jit(solution)/shard_map/all_to_all | solution.py:47
  75.6 1.5 %collective-permute-start.2 = (bf16[128,768]{1,0:T(8,128)(2,1)S(1)}, bf16[128,768]{1,0:T(8,128)(2,1)S(1)}, u32[]{:S(2)}, u32[]{:S(2)}) collective-permute-start(bf16[128,768]{1,0:T(8,128)(2,1)S(1)} %copy-done.6), channel_id=1, source_target_pairs={{0,32},{32,0},{1,33},{33,1},{2,34},{34,2},{3,35},{35,3},{4,36},{36... | collective-permute-start | bytes 589832 | tf_op jit(solution)/shard_map/ppermute | solution.py:53

commit v5 on v4

--- a/solution.py
+++ b/solution.py
@@ -153,9 +153,12 @@
 
 
 def logits_kernel(
-    block, own_ref, weight_ref, other_weight_ref, id_ref, mask_ref, advantage_ref, logits_ref, stats_ref, token_ref
+    block, own_ref, weight_ref, other_weight_ref, id_ref, mask_ref, advantage_ref,
+    logits_ref, stats_ref, token_ref, rows_ref, sem,
 ):
     depth, columns = weight_ref.shape
+    leave = pltpu.make_async_copy(own_ref.at[:, pl.ds(0, depth)], rows_ref, sem)
+    leave.start()
     for side, w_ref in enumerate((weight_ref, other_weight_ref)):
         here = slice(side * columns, (side + 1) * columns)
         for step in range(depth // block):
@@ -175,6 +178,7 @@
     lane = lax.broadcasted_iota(jnp.int32, (HALF, HALF), 1)
     tile = jnp.where(lane == 0, top, jnp.where(lane == 1, total, cross)).T[:8]
     stats_ref[...] = jnp.broadcast_to(tile[None], stats_ref.shape)
+    leave.wait()
 
 
 def local_logits(own, weight, other_weight, tokens, peers, block=1024):
@@ -186,9 +190,11 @@
             jax.ShapeDtypeStruct((HALF, 2 * columns), jnp.float32),
             jax.ShapeDtypeStruct((peers, 8, HALF), jnp.float32),
             jax.ShapeDtypeStruct((8, HALF), jnp.float32),
+            pltpu.HBM((HALF, depth), own.dtype),
         ),
         in_specs=[vmem] * 6,
-        out_specs=(vmem,) * 3,
+        out_specs=(vmem, vmem, vmem, pl.BlockSpec(memory_space=pltpu.HBM)),
+        scratch_shapes=[pltpu.SemaphoreType.DMA],
         compiler_params=pltpu.CompilerParams(vmem_limit_bytes=16 * MIB),
         cost_estimate=pl.CostEstimate(
             flops=4 * HALF * depth * columns, bytes_accessed=4 * depth * columns, transcendentals=0
@@ -275,40 +281,20 @@
     return parts[0]
 
 
-def sum_far_kernel(block, part_ref, out_ref, here_ref, sems):
-    steps = part_ref.shape[2] // block
-
-    def load(step):
-        columns = pl.ds(step * block, block)
-        return pltpu.make_async_copy(part_ref.at[:, :, columns], here_ref.at[:, :, columns], sems.at[step])
-
-    for step in range(steps):
-        load(step).start()
-    for step in range(steps):
-        load(step).wait()
-        columns = slice(step * block, (step + 1) * block)
-        total = total_of([here_ref[peer, :, columns] for peer in range(PEERS)])
-        out_ref[:, columns] = total.astype(out_ref.dtype)
-
-
 def sum_kernel(part_ref, out_ref):
     out_ref[...] = total_of([part_ref[peer] for peer in range(PEERS)]).astype(out_ref.dtype)
 
 
-def add_up(parts, block=None):
+def add_up(parts):
     vmem = pl.BlockSpec(memory_space=pltpu.VMEM)
-    space = pltpu.HBM if block else pltpu.VMEM
-    return pl.pallas_call(
-        functools.partial(sum_far_kernel, block) if block else sum_kernel,
+    return pl.pallas_call(
+        sum_kernel,
         out_shape=jax.ShapeDtypeStruct(parts.shape[1:], parts.dtype),
-        in_specs=[pl.BlockSpec(memory_space=space)],
+        in_specs=[vmem],
         out_specs=vmem,
-        scratch_shapes=(
-            [pltpu.VMEM(parts.shape, parts.dtype), pltpu.SemaphoreType.DMA((parts.shape[2] // block,))] if block else []
-        ),
         compiler_params=pltpu.CompilerParams(vmem_limit_bytes=8 * MIB),
         name="add_up",
-    )(pltpu.with_memory_space_constraint(parts, space))
+    )(pltpu.with_memory_space_constraint(parts, pltpu.VMEM))
 
 
 def head_grad_kernel(own_ref, other_ref, own_grad_ref, other_grad_ref, out_ref):
@@ -348,17 +334,17 @@
 
     tokens = (token_ids, response_mask, advantages)
     near = pltpu.with_memory_space_constraint(own, pltpu.VMEM)
-    logits, stats, token = local_logits(near, weight, other_weight, tokens, 64)
+    logits, stats, token, rows = local_logits(near, weight, other_weight, tokens, 64)
     stats = lax.all_to_all(stats, CHIPS, split_axis=0, concat_axis=0, tiled=True)
-    late, stats = lax.optimization_barrier((own, stats))
-    other = swap_cores(late)
+    rows, stats = lax.optimization_barrier((rows, stats))
+    other = swap_cores(rows)
 
     grad, theirs, part = hidden_grad(logits, near, stats, token, weight, other_weight)
-    grad_head = head_grad(own, other, grad, swap_cores(theirs), depth)
+    grad_head = head_grad(rows, other, grad, swap_cores(theirs), depth)
 
     part = exchange(part.reshape(PEERS, PEERS * ROWS, depth), SECOND)
     part, grad_head = lax.optimization_barrier((part, grad_head))
-    part = add_up(part, 1792)
+    part = add_up(part)
     grad_hidden = add_up(exchange(part.reshape(PEERS, ROWS, depth), FIRST))
     return grad_hidden, grad_head
 

time: 105 us -> 103 us (0.981)
    pallas_call x2, Pallas kernels: 2.2 us -> 0.9 us  [add_up(): pl.pallas_call(sum_kernel, out_shape=jax.ShapeDtypeStruct(parts.shape[1:]...]
where the time goes in v5:
time: 103 us
  blocking collectives  66 us (64%)
  Pallas kernels  21.4 us (21%)
  starting transfers between devices  8.38 us (8%)
  waiting for transfers between devices  5.49 us (5%)
    all_to_all x3, blocking collectives, exchange(): lax.all_to_all(x, AXES, split_axis=0, concat_axis=0, axis_index_groups=gr...  52.9 us
    all_to_all x1, blocking collectives, local(): lax.all_to_all(stats, CHIPS, split_axis=0, concat_axis=0, tiled=True)  13.1 us
    pallas_call x1, Pallas kernels, head_grad(): pl.pallas_call(head_grad_kernel, out_shape=jax.ShapeDtypeStruct((depth, c...  7.98 us
    pallas_call x1, Pallas kernels, hidden_grad(): pl.pallas_call(functools.partial(hidden_grad_kernel, block), out_shape=(p...  7.31 us
    ppermute x3, starting transfers between devices, swap_cores(): return lax.ppermute(x, 'core', [(0, 1), (1, 0)])  4.65 us
    all_to_all x1, waiting for transfers between devices, exchange(): lax.all_to_all(x, AXES, split_axis=0, concat_axis=0, axis_index_groups=gr...  4.06 us
    pallas_call x1, Pallas kernels, local_logits(): pl.pallas_call(functools.partial(logits_kernel, block), out_shape=(jax.Sh...  3.79 us
    all_to_all x1, starting transfers between devices, exchange(): lax.all_to_all(x, AXES, split_axis=0, concat_axis=0, axis_index_groups=gr...  3.74 us
  transfers between devices with their start and end apart: 4, of which 2 were waited for; matrix products, arithmetic and copies ran while one was open for 0% of the time, Pallas kernels for 16%

profile of v5, /device:TPU:1, one launch (start us, length us, event | category | flops | bytes accessed | tf_op | source)
XLA Modules:
  0.0 102.5 jit_solution(7220875204502551636)
XLA Ops:
  0.6 1.5 %collective-permute-start = (bf16[7168,768]{1,0:T(8,128)(2,1)}, bf16[7168,768]{1,0:T(8,128)(2,1)S(1)}, u32[]{:S(2)}, u32[]{:S(2)}) collective-permute-start(bf16[7168,768]{1,0:T(8,128)(2,1)} %weight_ref.3), channel_id=1, source_target_pairs={{0,32},{32,0},{1,33},{33,1},{2,34},{34,2},{3,35},{35,3},{4,36},{36... | collective-permute-start | bytes 33030152 | tf_op jit(solution)/shard_map/ppermute | solution.py:53
  2.1 1.1 %pack.1 = bf16[8,2,19456]{2,1,0:T(2,128)(2,1)S(1)} custom-call(bf16[2,7168]{1,0:T(2,128)(2,1)} %hidden_ref.1, bf16[2,98304]{1,0:T(2,128)(2,1)} %ref_ref.1), custom_call_target="tpu_custom_call" | custom-call | tf_op jit(solution)/shard_map/pack/pallas_call | solution.py:78
  3.2 20.8 %all_to_all.25.in_ref = bf16[8,2,19456]{2,1,0:T(2,128)(2,1)S(1)} all-to-all(bf16[8,2,19456]{2,1,0:T(2,128)(2,1)S(1)} %pack.1), channel_id=1, replica_groups={{0,1,4,5,8,9,12,13},{3,2,7,6,11,10,15,14},{68,69,64,65,76,77,72,73},{71..., dimensions={0} | all-to-all | bytes 1245184 | tf_op jit(solution)/shard_map/all_to_all | solution.py:47
  24.0 0.4 spread.1
  24.4 0.2 broadcast_in_dim.2
  24.6 0.2 pad_maximum_fusion
  24.8 0.0 copy-start.2
  24.8 0.0 copy-start.3
  24.8 0.0 copy-start.4
  24.8 19.4 %all_to_all.26 = bf16[8,16,8704]{2,1,0:T(8,128)(2,1)S(1)} all-to-all(bf16[8,16,8704]{2,1,0:T(8,128)(2,1)S(1)} %pad_maximum_fusion), channel_id=1, replica_groups={{0,3,68,71,24,27,92,95},{1,2,69,70,25,26,93,94},{4,7,64,67,28,31,88,91}..., dimensions={0} | all-to-all | bytes 4456448 | tf_op jit(solution)/shard_map/all_to_all | solution.py:47
  44.3 3.8 %logits.1 = (f32[128,1536]{1,0:T(8,128)S(1)}, f32[64,8,128]{2,1,0:T(8,128)S(1)}, f32[8,128]{1,0:T(8,128)S(1)}, bf16[128,7168]{1,0:T(8,128)(2,1)}) custom-call(bf16[128,8704]{1,0:T(8,128)(2,1)S(1)} %bitcast.5, bf16[7168,768]{1,0:T(8,128)(2,1)S(1)} %copy-done, bf16[7168,768]{1,0:T(8,128)(2,1)S(1)} %collective-permute-done.other_weight_ref, ...), custom_call_target="tpu_custom_call" | custom-call | flops 2818572288 | bytes 22020096 | tf_op jit(solution)/shard_map/logits/pallas_call | solution.py:187
  48.1 13.1 %all_to_all.27.stats_ref = f32[64,8,128]{2,1,0:T(8,128)S(1)} all-to-all(f32[64,8,128]{2,1,0:T(8,128)S(1)} %get-tuple-element.19), channel_id=1, replica_groups=mesh['yh'=2,'core'=2,'x'=4,'yl'=2,'z'=4] {'yh','x','yl','z'}, dimensions={0} | all-to-all | bytes 524288 | tf_op jit(solution)/shard_map/all_to_all | solution.py:338
  61.1 3.1 %collective-permute-start.1 = (bf16[128,7168]{1,0:T(8,128)(2,1)}, bf16[128,7168]{1,0:T(8,128)(2,1)}, u32[]{:S(2)}, u32[]{:S(2)}) collective-permute-start(bf16[128,7168]{1,0:T(8,128)(2,1)} %get-tuple-element.23.own_ref), channel_id=1, source_target_pairs={{0,32},{32,0},{1,33},{33,1},{2,34},{34,2},{3,35},{35,3},{4,36},{36... | collective-permute-start | bytes 5505032 | tf_op jit(solution)/shard_map/ppermute | solution.py:53
  64.2 7.3 %hidden_grad.1 = (bf16[128,768]{1,0:T(8,128)(2,1)}, bf16[128,768]{1,0:T(8,128)(2,1)}, bf16[128,7168]{1,0:T(8,128)(2,1)}) custom-call(f32[128,1536]{1,0:T(8,128)S(1)} %get-tuple-element.17.logits_ref, bf16[128,8704]{1,0:T(8,128)(2,1)S(1)} %bitcast.6, f32[64,8,128]{2,1,0:T(8,128)S(1)} %all_to_all.27.stats_ref, f32[8,128]{1,0:T(8,128)S(1)} %get-tuple-element.21.token_ref, ...), custom_call_target="tpu_custom_call" | custom-call | flops 5637144576 | bytes 22020096 | tf_op jit(solution)/shard_map/hidden_grad/pallas_call | solution.py:258
  71.5 0.0 copy-start.1
  71.5 3.7 %all-to-all-start.3 = ((bf16[8,16,7168]{2,1,0:T(8,128)(2,1)}), bf16[8,16,7168]{2,1,0:T(8,128)(2,1)S(1)}, u32[]{:S(2)}, u32[]{:S(2)}) async-start(bf16[8,16,7168]{2,1,0:T(8,128)(2,1)} %bitcast.10), calls=%async_computation.3 | async-start | bytes 3670016 | tf_op jit(solution)/shard_map/all_to_all | solution.py:47
  75.3 0.1 collective-permute-start.2
  75.4 1.4 %collective-permute-done.2.other_grad_ref = bf16[128,768]{1,0:T(8,128)(2,1)S(1)} collective-permute-done((bf16[128,768]{1,0:T(8,128)(2,1)S(1)}, bf16[128,768]{1,0:T(8,128)(2,1)S(1)}, u32[]{:S(2)}, u32[]{:S(2)}) %collective-permute-start.2) | collective-permute-done | bytes 196640 | tf_op jit(solution)/shard_map/ppermute | solution.py:53
  76.8 8.0 %head_grad.1 = bf16[7168,768]{1,0:T(8,128)(2,1)} custom-call(bf16[128,7168]{1,0:T(8,128)(2,1)} %get-tuple-element.23.own_ref, bf16[128,7168]{1,0:T(8,128)(2,1)} %collective-permute-done.1.other_ref, bf16[128,768]{1,0:T(8,128)(2,1)S(1)} %copy-done.1, bf16[128,768]{1,0:T(8,128)(2,1)S(1)} %collective-permute-done.2.other_grad_ref), custom_call_target="tpu_custom_call" | custom-call | flops 2818572288 | bytes 14680064 | tf_op jit(solution)/shard_map/head_grad/pallas_call | solution.py:312
  84.8 4.1 %all-to-all-done.3.part_ref = bf16[8,16,7168]{2,1,0:T(8,128)(2,1)S(1)} async-done(((bf16[8,16,7168]{2,1,0:T(8,128)(2,1)}), bf16[8,16,7168]{2,1,0:T(8,128)(2,1)S(1)}, u32[]{:S(2)}, u32[]{:S(2)}) %all-to-all-start.3) | async-done | bytes 1835040 | tf_op jit(solution)/shard_map/all_to_all | solution.py:47
  88.9 0.2 add_up.2
  89.1 0.1 reshape.28
  89.2 12.6 %all_to_all.28.part_ref = bf16[8,2,7168]{2,1,0:T(2,128)(2,1)S(1)} all-to-all(bf16[8,2,7168]{2,1,0:T(2,128)(2,1)S(1)} %reshape.28), channel_id=1, replica_groups={{0,1,4,5,8,9,12,13},{3,2,7,6,11,10,15,14},{68,69,64,65,76,77,72,73},{71..., dimensions={0} | all-to-all | bytes 458752 | tf_op jit(solution)/shard_map/all_to_all | solution.py:47
  101.8 0.7 add_up.3
  (10 shorter events, 0.0 us)
Async XLA Ops:
  0.6 43.6 %collective-permute-start = (bf16[7168,768]{1,0:T(8,128)(2,1)}, bf16[7168,768]{1,0:T(8,128)(2,1)S(1)}, u32[]{:S(2)}, u32[]{:S(2)}) collective-permute-start(bf16[7168,768]{1,0:T(8,128)(2,1)} %weight_ref.3), channel_id=1, source_target_pairs={{0,32},{32,0},{1,33},{33,1},{2,34},{34,2},{3,35},{35,3},{4,36},{36... | collective-permute-start | bytes 33030152 | tf_op jit(solution)/shard_map/ppermute | solution.py:53
  24.0 20.2 %copy-start = (bf16[7168,768]{1,0:T(8,128)(2,1)S(1)}, bf16[7168,768]{1,0:T(8,128)(2,1)}, u32[]{:S(2)}) copy-start(bf16[7168,768]{1,0:T(8,128)(2,1)} %weight_ref.3) | copy-start | bytes 33030148
  24.8 19.5 %copy-start.2 = (s32[256]{0:T(256)S(1)}, s32[256]{0:T(256)}, u32[]{:S(2)}) copy-start(s32[256]{0:T(256)} %param.9) | copy-start | bytes 3076
  24.8 19.5 %copy-start.3 = (s32[256]{0:T(256)S(1)}, s32[256]{0:T(256)}, u32[]{:S(2)}) copy-start(s32[256]{0:T(256)} %param.10) | copy-start | bytes 3076
  24.8 19.5 %copy-start.4 = (f32[256]{0:T(256)S(1)}, f32[256]{0:T(256)}, u32[]{:S(2)}) copy-start(f32[256]{0:T(256)} %param.11) | copy-start | bytes 3076
  61.1 15.7 %collective-permute-start.1 = (bf16[128,7168]{1,0:T(8,128)(2,1)}, bf16[128,7168]{1,0:T(8,128)(2,1)}, u32[]{:S(2)}, u32[]{:S(2)}) collective-permute-start(bf16[128,7168]{1,0:T(8,128)(2,1)} %get-tuple-element.23.own_ref), channel_id=1, source_target_pairs={{0,32},{32,0},{1,33},{33,1},{2,34},{34,2},{3,35},{35,3},{4,36},{36... | collective-permute-start | bytes 5505032 | tf_op jit(solution)/shard_map/ppermute | solution.py:53
  71.5 3.8 %copy-start.5 = (bf16[128,768]{1,0:T(8,128)(2,1)S(1)}, bf16[128,768]{1,0:T(8,128)(2,1)}, u32[]{:S(2)}) copy-start(bf16[128,768]{1,0:T(8,128)(2,1)} %get-tuple-element.25) | copy-start | bytes 589828
  71.5 5.3 %copy-start.1 = (bf16[128,768]{1,0:T(8,128)(2,1)S(1)}, bf16[128,768]{1,0:T(8,128)(2,1)}, u32[]{:S(2)}) copy-start(bf16[128,768]{1,0:T(8,128)(2,1)} %get-tuple-element.24.own_grad_ref) | copy-start | bytes 589828
  71.5 17.3 %all-to-all-start.3 = ((bf16[8,16,7168]{2,1,0:T(8,128)(2,1)}), bf16[8,16,7168]{2,1,0:T(8,128)(2,1)S(1)}, u32[]{:S(2)}, u32[]{:S(2)}) async-start(bf16[8,16,7168]{2,1,0:T(8,128)(2,1)} %bitcast.10), calls=%async_computation.3 | async-start | bytes 3670016 | tf_op jit(solution)/shard_map/all_to_all | solution.py:47
  75.3 1.5 %collective-permute-start.2 = (bf16[128,768]{1,0:T(8,128)(2,1)S(1)}, bf16[128,768]{1,0:T(8,128)(2,1)S(1)}, u32[]{:S(2)}, u32[]{:S(2)}) collective-permute-start(bf16[128,768]{1,0:T(8,128)(2,1)S(1)} %copy-done.5), channel_id=1, source_target_pairs={{0,32},{32,0},{1,33},{33,1},{2,34},{34,2},{3,35},{35,3},{4,36},{36... | collective-permute-start | bytes 589832 | tf_op jit(solution)/shard_map/ppermute | solution.py:53

commit v6 on v5

--- a/solution.py
+++ b/solution.py
@@ -154,11 +154,16 @@
 
 def logits_kernel(
     block, own_ref, weight_ref, other_weight_ref, id_ref, mask_ref, advantage_ref,
-    logits_ref, stats_ref, token_ref, rows_ref, sem,
+    logits_ref, stats_ref, token_ref, low_ref, high_ref, sems,
 ):
     depth, columns = weight_ref.shape
-    leave = pltpu.make_async_copy(own_ref.at[:, pl.ds(0, depth)], rows_ref, sem)
-    leave.start()
+    half = HALF // 2
+    leave = [
+        pltpu.make_async_copy(own_ref.at[pl.ds(i * half, half), pl.ds(0, depth)], ref, sems.at[i])
+        for i, ref in enumerate((low_ref, high_ref))
+    ]
+    for copy in leave:
+        copy.start()
     for side, w_ref in enumerate((weight_ref, other_weight_ref)):
         here = slice(side * columns, (side + 1) * columns)
         for step in range(depth // block):
@@ -178,7 +183,8 @@
     lane = lax.broadcasted_iota(jnp.int32, (HALF, HALF), 1)
     tile = jnp.where(lane == 0, top, jnp.where(lane == 1, total, cross)).T[:8]
     stats_ref[...] = jnp.broadcast_to(tile[None], stats_ref.shape)
-    leave.wait()
+    for copy in leave:
+        copy.wait()
 
 
 def local_logits(own, weight, other_weight, tokens, peers, block=1024):
@@ -190,11 +196,12 @@
             jax.ShapeDtypeStruct((HALF, 2 * columns), jnp.float32),
             jax.ShapeDtypeStruct((peers, 8, HALF), jnp.float32),
             jax.ShapeDtypeStruct((8, HALF), jnp.float32),
-            pltpu.HBM((HALF, depth), own.dtype),
+            pltpu.HBM((HALF // 2, depth), own.dtype),
+            pltpu.HBM((HALF // 2, depth), own.dtype),
         ),
         in_specs=[vmem] * 6,
-        out_specs=(vmem, vmem, vmem, pl.BlockSpec(memory_space=pltpu.HBM)),
-        scratch_shapes=[pltpu.SemaphoreType.DMA],
+        out_specs=(vmem,) * 3 + (pl.BlockSpec(memory_space=pltpu.HBM),) * 2,
+        scratch_shapes=[pltpu.SemaphoreType.DMA((2,))],
         compiler_params=pltpu.CompilerParams(vmem_limit_bytes=16 * MIB),
         cost_estimate=pl.CostEstimate(
             flops=4 * HALF * depth * columns, bytes_accessed=4 * depth * columns, transcendentals=0
@@ -297,30 +304,30 @@
     )(pltpu.with_memory_space_constraint(parts, pltpu.VMEM))
 
 
-def head_grad_kernel(own_ref, other_ref, own_grad_ref, other_grad_ref, out_ref):
-    x = jnp.concatenate([own_ref[...], other_ref[...]], axis=0)
+def head_grad_kernel(a_ref, b_ref, c_ref, d_ref, own_grad_ref, other_grad_ref, out_ref):
+    x = jnp.concatenate([ref[...] for ref in (a_ref, b_ref, c_ref, d_ref)], axis=0)
     grad = jnp.concatenate([own_grad_ref[...], other_grad_ref[...]], axis=0)
     out_ref[...] = lax.dot_general(
         x, grad, (((0,), (0,)), ((), ())), preferred_element_type=jnp.float32
     ).astype(out_ref.dtype)
 
 
-def head_grad(own, other, own_grad, other_grad, depth, block=1792):
+def head_grad(rows, own_grad, other_grad, depth, block=1792):
     tokens, columns = own_grad.shape
-    x_spec = pl.BlockSpec((HALF, block), lambda k: (0, k))
+    x_spec = pl.BlockSpec((HALF // 2, block), lambda k: (0, k))
     grad_spec = pl.BlockSpec(own_grad.shape, lambda k: (0, 0))
     return pl.pallas_call(
         head_grad_kernel,
         out_shape=jax.ShapeDtypeStruct((depth, columns), own_grad.dtype),
         grid=(depth // block,),
-        in_specs=[x_spec, x_spec, grad_spec, grad_spec],
+        in_specs=[x_spec] * 4 + [grad_spec] * 2,
         out_specs=pl.BlockSpec((block, columns), lambda k: (k, 0)),
         compiler_params=pltpu.CompilerParams(vmem_limit_bytes=16 * MIB),
         cost_estimate=pl.CostEstimate(
             flops=4 * tokens * depth * columns, bytes_accessed=2 * depth * (columns + 2 * tokens), transcendentals=0
         ),
         name="head_grad",
-    )(*(pltpu.with_memory_space_constraint(x, pltpu.HBM) for x in (own, other)), own_grad, other_grad)
+    )(*(pltpu.with_memory_space_constraint(x, pltpu.HBM) for x in rows), own_grad, other_grad)
 
 
 def local(hidden, head_weight, ref_logprobs, token_ids, response_mask, advantages):
@@ -334,13 +341,12 @@
 
     tokens = (token_ids, response_mask, advantages)
     near = pltpu.with_memory_space_constraint(own, pltpu.VMEM)
-    logits, stats, token, rows = local_logits(near, weight, other_weight, tokens, 64)
+    logits, stats, token, *rows = local_logits(near, weight, other_weight, tokens, 64)
     stats = lax.all_to_all(stats, CHIPS, split_axis=0, concat_axis=0, tiled=True)
-    rows, stats = lax.optimization_barrier((rows, stats))
-    other = swap_cores(rows)
 
     grad, theirs, part = hidden_grad(logits, near, stats, token, weight, other_weight)
-    grad_head = head_grad(rows, other, grad, swap_cores(theirs), depth)
+    *late, theirs = lax.optimization_barrier((*rows, theirs))
+    grad_head = head_grad((*rows, *map(swap_cores, late)), grad, swap_cores(theirs), depth)
 
     part = exchange(part.reshape(PEERS, PEERS * ROWS, depth), SECOND)
     part, grad_head = lax.optimization_barrier((part, grad_head))

time: 103 us -> 107 us (1.039)
  blocking collectives: 66 us -> 70.4 us
  waiting for transfers between devices: 5.49 us -> 3.39 us
    all_to_all x3, blocking collectives: 52.9 us -> 57.3 us  [exchange(): lax.all_to_all(x, AXES, split_axis=0, concat_axis=0, axis_index_groups=gr...]
    all_to_all x1, waiting for transfers between devices: 4.06 us -> 0.01 us  [exchange(): lax.all_to_all(x, AXES, split_axis=0, concat_axis=0, axis_index_groups=gr...]
    ppermute x3 -> x4, waiting for transfers between devices: 1.43 us -> 3.39 us  [swap_cores(): return lax.ppermute(x, 'core', [(0, 1), (1, 0)])]
    ppermute x3 -> x4, starting transfers between devices: 4.65 us -> 5.15 us  [swap_cores(): return lax.ppermute(x, 'core', [(0, 1), (1, 0)])]
  transfers between devices with their start and end apart: 4 -> 5, of which waited for: 2 -> 2; matrix products, arithmetic and copies ran while one was open for 0% -> 0% of each run, Pallas kernels for 16% -> 9%
where the time goes in v6:
time: 107 us
  blocking collectives  70.4 us (66%)
  Pallas kernels  22 us (21%)
  starting transfers between devices  8.89 us (8%)
  waiting for transfers between devices  3.39 us (3%)
  local copies, waits for them, and re-layouts  1.28 us (1%)
    all_to_all x3, blocking collectives, exchange(): lax.all_to_all(x, AXES, split_axis=0, concat_axis=0, axis_index_groups=gr...  57.3 us
    all_to_all x1, blocking collectives, local(): lax.all_to_all(stats, CHIPS, split_axis=0, concat_axis=0, tiled=True)  13.1 us
    pallas_call x1, Pallas kernels, head_grad(): pl.pallas_call(head_grad_kernel, out_shape=jax.ShapeDtypeStruct((depth, c...  8.13 us
    pallas_call x1, Pallas kernels, hidden_grad(): pl.pallas_call(functools.partial(hidden_grad_kernel, block), out_shape=(p...  7.31 us
    ppermute x4, starting transfers between devices, swap_cores(): return lax.ppermute(x, 'core', [(0, 1), (1, 0)])  5.15 us
    pallas_call x1, Pallas kernels, local_logits(): pl.pallas_call(functools.partial(logits_kernel, block), out_shape=(jax.Sh...  4.2 us
    all_to_all x1, starting transfers between devices, exchange(): lax.all_to_all(x, AXES, split_axis=0, concat_axis=0, axis_index_groups=gr...  3.74 us
    ppermute x4, waiting for transfers between devices, swap_cores(): return lax.ppermute(x, 'core', [(0, 1), (1, 0)])  3.39 us
  transfers between devices with their start and end apart: 5, of which 2 were waited for; matrix products, arithmetic and copies ran while one was open for 0% of the time, Pallas kernels for 9%

profile of v6, /device:TPU:1, one launch (start us, length us, event | category | flops | bytes accessed | tf_op | source)
XLA Modules:
  0.0 106.9 jit_solution(7844539394678395433)
XLA Ops:
  0.6 1.5 %collective-permute-start = (bf16[7168,768]{1,0:T(8,128)(2,1)}, bf16[7168,768]{1,0:T(8,128)(2,1)S(1)}, u32[]{:S(2)}, u32[]{:S(2)}) collective-permute-start(bf16[7168,768]{1,0:T(8,128)(2,1)} %weight_ref.3), channel_id=1, source_target_pairs={{0,32},{32,0},{1,33},{33,1},{2,34},{34,2},{3,35},{35,3},{4,36},{36... | collective-permute-start | bytes 33030152 | tf_op jit(solution)/shard_map/ppermute | solution.py:53
  2.1 1.1 %pack.1 = bf16[8,2,19456]{2,1,0:T(2,128)(2,1)S(1)} custom-call(bf16[2,7168]{1,0:T(2,128)(2,1)} %hidden_ref.1, bf16[2,98304]{1,0:T(2,128)(2,1)} %ref_ref.1), custom_call_target="tpu_custom_call" | custom-call | tf_op jit(solution)/shard_map/pack/pallas_call | solution.py:78
  3.2 20.8 %all_to_all.25.in_ref = bf16[8,2,19456]{2,1,0:T(2,128)(2,1)S(1)} all-to-all(bf16[8,2,19456]{2,1,0:T(2,128)(2,1)S(1)} %pack.1), channel_id=1, replica_groups={{0,1,4,5,8,9,12,13},{3,2,7,6,11,10,15,14},{68,69,64,65,76,77,72,73},{71..., dimensions={0} | all-to-all | bytes 1245184 | tf_op jit(solution)/shard_map/all_to_all | solution.py:47
  24.0 0.4 spread.1
  24.4 0.2 broadcast_in_dim.2
  24.6 0.2 pad_maximum_fusion
  24.8 0.0 copy-start.2
  24.8 19.4 %all_to_all.26 = bf16[8,16,8704]{2,1,0:T(8,128)(2,1)S(1)} all-to-all(bf16[8,16,8704]{2,1,0:T(8,128)(2,1)S(1)} %pad_maximum_fusion), channel_id=1, replica_groups={{0,3,68,71,24,27,92,95},{1,2,69,70,25,26,93,94},{4,7,64,67,28,31,88,91}..., dimensions={0} | all-to-all | bytes 4456448 | tf_op jit(solution)/shard_map/all_to_all | solution.py:47
  44.3 4.2 %logits.1 = (f32[128,1536]{1,0:T(8,128)S(1)}, f32[64,8,128]{2,1,0:T(8,128)S(1)}, f32[8,128]{1,0:T(8,128)S(1)}, bf16[64,7168]{1,0:T(8,128)(2,1)}, bf16[64,7168]{1,0:T(8,128)(2,1)}) custom-call(bf16[128,8704]{1,0:T(8,128)(2,1)S(1)} %bitcast.5, bf16[7168,768]{1,0:T(8,128)(2,1)S(1)} %copy-done, bf16[7168,768]{1,0:T(8,128)(2,1)S(1)} %collective-permute-done.other_weight_ref, ...), custom_call_target="tpu_custom_call" | custom-call | flops 2818572288 | bytes 22020096 | tf_op jit(solution)/shard_map/logits/pallas_call | solution.py:193
  48.5 13.1 %all_to_all.27.stats_ref = f32[64,8,128]{2,1,0:T(8,128)S(1)} all-to-all(f32[64,8,128]{2,1,0:T(8,128)S(1)} %get-tuple-element.20), channel_id=1, replica_groups=mesh['yh'=2,'core'=2,'x'=4,'yl'=2,'z'=4] {'yh','x','yl','z'}, dimensions={0} | all-to-all | bytes 524288 | tf_op jit(solution)/shard_map/all_to_all | solution.py:345
  61.6 7.3 %hidden_grad.1 = (bf16[128,768]{1,0:T(8,128)(2,1)}, bf16[128,768]{1,0:T(8,128)(2,1)}, bf16[128,7168]{1,0:T(8,128)(2,1)}) custom-call(f32[128,1536]{1,0:T(8,128)S(1)} %get-tuple-element.19.logits_ref, bf16[128,8704]{1,0:T(8,128)(2,1)S(1)} %bitcast.6, f32[64,8,128]{2,1,0:T(8,128)S(1)} %all_to_all.27.stats_ref, f32[8,128]{1,0:T(8,128)S(1)} %get-tuple-element.21.token_ref, ...), custom_call_target="tpu_custom_call" | custom-call | flops 5637144576 | bytes 22020096 | tf_op jit(solution)/shard_map/hidden_grad/pallas_call | solution.py:265
  68.9 3.7 %all-to-all-start.3 = ((bf16[8,16,7168]{2,1,0:T(8,128)(2,1)}), bf16[8,16,7168]{2,1,0:T(8,128)(2,1)S(1)}, u32[]{:S(2)}, u32[]{:S(2)}) async-start(bf16[8,16,7168]{2,1,0:T(8,128)(2,1)} %bitcast.10), calls=%async_computation.3 | async-start | bytes 3670016 | tf_op jit(solution)/shard_map/all_to_all | solution.py:47
  72.7 3.1 %collective-permute-start.1 = (bf16[64,7168]{1,0:T(8,128)(2,1)S(1)}, bf16[64,7168]{1,0:T(8,128)(2,1)S(1)}, u32[]{:S(2)}, u32[]{:S(2)}) collective-permute-start(bf16[64,7168]{1,0:T(8,128)(2,1)S(1)} %copy-done.5), channel_id=1, source_target_pairs={{0,32},{32,0},{1,33},{33,1},{2,34},{34,2},{3,35},{35,3},{4,36},{36... | collective-permute-start | bytes 2752520 | tf_op jit(solution)/shard_map/ppermute | solution.py:53
  75.8 0.1 collective-permute-start.2
  75.9 0.4 collective-permute-start.3
  76.3 2.5 %collective-permute-done.3.other_grad_ref = bf16[128,768]{1,0:T(8,128)(2,1)S(1)} collective-permute-done((bf16[128,768]{1,0:T(8,128)(2,1)S(1)}, bf16[128,768]{1,0:T(8,128)(2,1)S(1)}, u32[]{:S(2)}, u32[]{:S(2)}) %collective-permute-start.3) | collective-permute-done | bytes 196640 | tf_op jit(solution)/shard_map/ppermute | solution.py:53
  78.8 0.9 collective-permute-done.2.d_ref
  79.7 0.1 copy-done.6
  79.8 0.9 copy-done.7
  80.7 8.1 %head_grad.1 = bf16[7168,768]{1,0:T(8,128)(2,1)} custom-call(bf16[64,7168]{1,0:T(8,128)(2,1)} %get-tuple-element.26.a_ref, bf16[64,7168]{1,0:T(8,128)(2,1)} %get-tuple-element.27.b_ref, bf16[64,7168]{1,0:T(8,128)(2,1)} %copy-done.6, bf16[64,7168]{1,0:T(8,128)(2,1)} %copy-done.7, bf16[128,768]{1,0:T(8,128)(2,1)S(1)} %copy-done.1, ...), custom_call_target="tpu_custom_call" | custom-call | flops 2818572288 | bytes 14680064 | tf_op jit(solution)/shard_map/head_grad/pallas_call | solution.py:319
  88.8 0.2 add_up.2
  89.1 0.1 reshape.28
  89.1 17.1 %all_to_all.28.part_ref = bf16[8,2,7168]{2,1,0:T(2,128)(2,1)S(1)} all-to-all(bf16[8,2,7168]{2,1,0:T(2,128)(2,1)S(1)} %reshape.28), channel_id=1, replica_groups={{0,1,4,5,8,9,12,13},{3,2,7,6,11,10,15,14},{68,69,64,65,76,77,72,73},{71..., dimensions={0} | all-to-all | bytes 458752 | tf_op jit(solution)/shard_map/all_to_all | solution.py:47
  106.2 0.7 add_up.3
  (18 shorter events, 0.0 us)
Async XLA Ops:
  0.6 43.6 %collective-permute-start = (bf16[7168,768]{1,0:T(8,128)(2,1)}, bf16[7168,768]{1,0:T(8,128)(2,1)S(1)}, u32[]{:S(2)}, u32[]{:S(2)}) collective-permute-start(bf16[7168,768]{1,0:T(8,128)(2,1)} %weight_ref.3), channel_id=1, source_target_pairs={{0,32},{32,0},{1,33},{33,1},{2,34},{34,2},{3,35},{35,3},{4,36},{36... | collective-permute-start | bytes 33030152 | tf_op jit(solution)/shard_map/ppermute | solution.py:53
  24.0 20.2 %copy-start = (bf16[7168,768]{1,0:T(8,128)(2,1)S(1)}, bf16[7168,768]{1,0:T(8,128)(2,1)}, u32[]{:S(2)}) copy-start(bf16[7168,768]{1,0:T(8,128)(2,1)} %weight_ref.3) | copy-start | bytes 33030148
  24.8 19.5 %copy-start.2 = (s32[256]{0:T(256)S(1)}, s32[256]{0:T(256)}, u32[]{:S(2)}) copy-start(s32[256]{0:T(256)} %param.9) | copy-start | bytes 3076
  24.8 19.5 %copy-start.3 = (s32[256]{0:T(256)S(1)}, s32[256]{0:T(256)}, u32[]{:S(2)}) copy-start(s32[256]{0:T(256)} %param.10) | copy-start | bytes 3076
  24.8 19.5 %copy-start.4 = (f32[256]{0:T(256)S(1)}, f32[256]{0:T(256)}, u32[]{:S(2)}) copy-start(f32[256]{0:T(256)} %param.11) | copy-start | bytes 3076
  68.9 3.8 %copy-start.5 = (bf16[64,7168]{1,0:T(8,128)(2,1)S(1)}, bf16[64,7168]{1,0:T(8,128)(2,1)}, u32[]{:S(2)}) copy-start(bf16[64,7168]{1,0:T(8,128)(2,1)} %get-tuple-element.26.a_ref) | copy-start | bytes 2752516
  68.9 7.0 %copy-start.8 = (bf16[128,768]{1,0:T(8,128)(2,1)S(1)}, bf16[128,768]{1,0:T(8,128)(2,1)}, u32[]{:S(2)}) copy-start(bf16[128,768]{1,0:T(8,128)(2,1)} %get-tuple-element.29) | copy-start | bytes 589828
  68.9 11.8 %copy-start.1 = (bf16[128,768]{1,0:T(8,128)(2,1)S(1)}, bf16[128,768]{1,0:T(8,128)(2,1)}, u32[]{:S(2)}) copy-start(bf16[128,768]{1,0:T(8,128)(2,1)} %get-tuple-element.28.own_grad_ref) | copy-start | bytes 589828
  68.9 19.9 %all-to-all-start.3 = ((bf16[8,16,7168]{2,1,0:T(8,128)(2,1)}), bf16[8,16,7168]{2,1,0:T(8,128)(2,1)S(1)}, u32[]{:S(2)}, u32[]{:S(2)}) async-start(bf16[8,16,7168]{2,1,0:T(8,128)(2,1)} %bitcast.10), calls=%async_computation.3 | async-start | bytes 3670016 | tf_op jit(solution)/shard_map/all_to_all | solution.py:47
  72.7 6.2 %collective-permute-start.1 = (bf16[64,7168]{1,0:T(8,128)(2,1)S(1)}, bf16[64,7168]{1,0:T(8,128)(2,1)S(1)}, u32[]{:S(2)}, u32[]{:S(2)}) collective-permute-start(bf16[64,7168]{1,0:T(8,128)(2,1)S(1)} %copy-done.5), channel_id=1, source_target_pairs={{0,32},{32,0},{1,33},{33,1},{2,34},{34,2},{3,35},{35,3},{4,36},{36... | collective-permute-start | bytes 2752520 | tf_op jit(solution)/shard_map/ppermute | solution.py:53
  75.8 3.9 %collective-permute-start.2 = (bf16[64,7168]{1,0:T(8,128)(2,1)}, bf16[64,7168]{1,0:T(8,128)(2,1)S(1)}, u32[]{:S(2)}, u32[]{:S(2)}) collective-permute-start(bf16[64,7168]{1,0:T(8,128)(2,1)} %get-tuple-element.27.b_ref), channel_id=1, source_target_pairs={{0,32},{32,0},{1,33},{33,1},{2,34},{34,2},{3,35},{35,3},{4,36},{36... | collective-permute-start | bytes 2752520 | tf_op jit(solution)/shard_map/ppermute | solution.py:53
  75.9 2.9 %collective-permute-start.3 = (bf16[128,768]{1,0:T(8,128)(2,1)S(1)}, bf16[128,768]{1,0:T(8,128)(2,1)S(1)}, u32[]{:S(2)}, u32[]{:S(2)}) collective-permute-start(bf16[128,768]{1,0:T(8,128)(2,1)S(1)} %copy-done.8), channel_id=1, source_target_pairs={{0,32},{32,0},{1,33},{33,1},{2,34},{34,2},{3,35},{35,3},{4,36},{36... | collective-permute-start | bytes 589832 | tf_op jit(solution)/shard_map/ppermute | solution.py:53
  78.8 0.9 copy-start.6
  79.7 1.0 copy-start.7

commit v7 on v5

--- a/solution.py
+++ b/solution.py
@@ -87,7 +87,7 @@
 
 
 def spread_kernel(columns, in_ref, rows_ref, lp_ref):
-    depth = rows_ref.shape[1]
+    depth = rows_ref.shape[2]
     first = in_ref.shape[2] - depth
 
     def rows(start, size):
@@ -96,7 +96,9 @@
 
     block = 512
     for start in range(0, depth, block):
-        rows_ref[:, start : start + block] = rows(first + start, block)
+        here = rows(first + start, block)
+        for peer in range(PEERS):
+            rows_ref[peer, :, start : start + block] = here
     for peer in range(PEERS):
         lp_ref[peer] = rows(peer * 2 * columns, 2 * columns)
 
@@ -106,7 +108,7 @@
     rows, lp = pl.pallas_call(
         functools.partial(spread_kernel, columns),
         out_shape=(
-            jax.ShapeDtypeStruct((PEERS * ROWS, depth), got.dtype),
+            jax.ShapeDtypeStruct((PEERS, PEERS * ROWS, depth), got.dtype),
             jax.ShapeDtypeStruct((PEERS, PEERS * ROWS, 2 * columns), got.dtype),
         ),
         in_specs=[vmem],
@@ -114,7 +116,6 @@
         compiler_params=pltpu.CompilerParams(vmem_limit_bytes=8 * MIB),
         name="spread",
     )(got)
-    rows = jnp.broadcast_to(rows[None], (PEERS,) + rows.shape)
     return jnp.concatenate([rows, lp], axis=2)
 
 

time: 103 us -> 103 us (level)
  no operation moved by 1% of the time
where the time goes in v7:
time: 103 us
  blocking collectives  65.8 us (64%)
  Pallas kernels  21.6 us (21%)
  starting transfers between devices  8.85 us (9%)
  waiting for transfers between devices  5.49 us (5%)
    all_to_all x3, blocking collectives, exchange(): lax.all_to_all(x, AXES, split_axis=0, concat_axis=0, axis_index_groups=gr...  52.8 us
    all_to_all x1, blocking collectives, local(): lax.all_to_all(stats, CHIPS, split_axis=0, concat_axis=0, tiled=True)  13 us
    pallas_call x1, Pallas kernels, head_grad(): pl.pallas_call(head_grad_kernel, out_shape=jax.ShapeDtypeStruct((depth, c...  7.98 us
    pallas_call x1, Pallas kernels, hidden_grad(): pl.pallas_call(functools.partial(hidden_grad_kernel, block), out_shape=(p...  7.31 us
    ppermute x3, starting transfers between devices, swap_cores(): return lax.ppermute(x, 'core', [(0, 1), (1, 0)])  5.11 us
    all_to_all x1, waiting for transfers between devices, exchange(): lax.all_to_all(x, AXES, split_axis=0, concat_axis=0, axis_index_groups=gr...  4.06 us
    pallas_call x1, Pallas kernels, local_logits(): pl.pallas_call(functools.partial(logits_kernel, block), out_shape=(jax.Sh...  3.79 us
    all_to_all x1, starting transfers between devices, exchange(): lax.all_to_all(x, AXES, split_axis=0, concat_axis=0, axis_index_groups=gr...  3.74 us
  transfers between devices with their start and end apart: 4, of which 2 were waited for; matrix products, arithmetic and copies ran while one was open for 0% of the time, Pallas kernels for 16%

profile of v7, /device:TPU:1, one launch (start us, length us, event | category | flops | bytes accessed | tf_op | source)
XLA Modules:
  0.0 102.8 jit_solution(1232140614124811149)
XLA Ops:
  0.6 1.5 %collective-permute-start = (bf16[7168,768]{1,0:T(8,128)(2,1)}, bf16[7168,768]{1,0:T(8,128)(2,1)S(1)}, u32[]{:S(2)}, u32[]{:S(2)}) collective-permute-start(bf16[7168,768]{1,0:T(8,128)(2,1)} %weight_ref.3), channel_id=1, source_target_pairs={{0,32},{32,0},{1,33},{33,1},{2,34},{34,2},{3,35},{35,3},{4,36},{36... | collective-permute-start | bytes 33030152 | tf_op jit(solution)/shard_map/ppermute | solution.py:53
  2.1 1.2 %pack.1 = bf16[8,2,19456]{2,1,0:T(2,128)(2,1)S(1)} custom-call(bf16[2,7168]{1,0:T(2,128)(2,1)} %hidden_ref.1, bf16[2,98304]{1,0:T(2,128)(2,1)} %ref_ref.1), custom_call_target="tpu_custom_call" | custom-call | tf_op jit(solution)/shard_map/pack/pallas_call | solution.py:78
  3.4 21.1 %all_to_all.25.in_ref = bf16[8,2,19456]{2,1,0:T(2,128)(2,1)S(1)} all-to-all(bf16[8,2,19456]{2,1,0:T(2,128)(2,1)S(1)} %pack.1), channel_id=1, replica_groups={{0,1,4,5,8,9,12,13},{3,2,7,6,11,10,15,14},{68,69,64,65,76,77,72,73},{71..., dimensions={0} | all-to-all | bytes 1245184 | tf_op jit(solution)/shard_map/all_to_all | solution.py:47
  24.4 0.4 spread.1
  24.9 0.2 pad_maximum_fusion
  25.0 0.0 copy-start.2
  25.0 0.0 copy-start.3
  25.1 0.0 copy-start.4
  25.1 19.0 %all_to_all.26 = bf16[8,16,8704]{2,1,0:T(8,128)(2,1)S(1)} all-to-all(bf16[8,16,8704]{2,1,0:T(8,128)(2,1)S(1)} %pad_maximum_fusion), channel_id=1, replica_groups={{0,3,68,71,24,27,92,95},{1,2,69,70,25,26,93,94},{4,7,64,67,28,31,88,91}..., dimensions={0} | all-to-all | bytes 4456448 | tf_op jit(solution)/shard_map/all_to_all | solution.py:47
  44.1 3.8 %logits.1 = (f32[128,1536]{1,0:T(8,128)S(1)}, f32[64,8,128]{2,1,0:T(8,128)S(1)}, f32[8,128]{1,0:T(8,128)S(1)}, bf16[128,7168]{1,0:T(8,128)(2,1)}) custom-call(bf16[128,8704]{1,0:T(8,128)(2,1)S(1)} %bitcast.5, bf16[7168,768]{1,0:T(8,128)(2,1)S(1)} %copy-done, bf16[7168,768]{1,0:T(8,128)(2,1)S(1)} %collective-permute-done.other_weight_ref, ...), custom_call_target="tpu_custom_call" | custom-call | flops 2818572288 | bytes 22020096 | tf_op jit(solution)/shard_map/logits/pallas_call | solution.py:188
  47.9 13.0 %all_to_all.27.stats_ref = f32[64,8,128]{2,1,0:T(8,128)S(1)} all-to-all(f32[64,8,128]{2,1,0:T(8,128)S(1)} %get-tuple-element.19), channel_id=1, replica_groups=mesh['yh'=2,'core'=2,'x'=4,'yl'=2,'z'=4] {'yh','x','yl','z'}, dimensions={0} | all-to-all | bytes 524288 | tf_op jit(solution)/shard_map/all_to_all | solution.py:339
  60.9 3.5 %collective-permute-start.1 = (bf16[128,7168]{1,0:T(8,128)(2,1)}, bf16[128,7168]{1,0:T(8,128)(2,1)}, u32[]{:S(2)}, u32[]{:S(2)}) collective-permute-start(bf16[128,7168]{1,0:T(8,128)(2,1)} %get-tuple-element.23.own_ref), channel_id=1, source_target_pairs={{0,32},{32,0},{1,33},{33,1},{2,34},{34,2},{3,35},{35,3},{4,36},{36... | collective-permute-start | bytes 5505032 | tf_op jit(solution)/shard_map/ppermute | solution.py:53
  64.5 7.3 %hidden_grad.1 = (bf16[128,768]{1,0:T(8,128)(2,1)}, bf16[128,768]{1,0:T(8,128)(2,1)}, bf16[128,7168]{1,0:T(8,128)(2,1)}) custom-call(f32[128,1536]{1,0:T(8,128)S(1)} %get-tuple-element.17.logits_ref, bf16[128,8704]{1,0:T(8,128)(2,1)S(1)} %bitcast.6, f32[64,8,128]{2,1,0:T(8,128)S(1)} %all_to_all.27.stats_ref, f32[8,128]{1,0:T(8,128)S(1)} %get-tuple-element.21.token_ref, ...), custom_call_target="tpu_custom_call" | custom-call | flops 5637144576 | bytes 22020096 | tf_op jit(solution)/shard_map/hidden_grad/pallas_call | solution.py:259
  71.8 0.0 copy-start.1
  71.8 3.7 %all-to-all-start.3 = ((bf16[8,16,7168]{2,1,0:T(8,128)(2,1)}), bf16[8,16,7168]{2,1,0:T(8,128)(2,1)S(1)}, u32[]{:S(2)}, u32[]{:S(2)}) async-start(bf16[8,16,7168]{2,1,0:T(8,128)(2,1)} %bitcast.10), calls=%async_computation.3 | async-start | bytes 3670016 | tf_op jit(solution)/shard_map/all_to_all | solution.py:47
  75.6 0.1 collective-permute-start.2
  75.7 1.4 %collective-permute-done.2.other_grad_ref = bf16[128,768]{1,0:T(8,128)(2,1)S(1)} collective-permute-done((bf16[128,768]{1,0:T(8,128)(2,1)S(1)}, bf16[128,768]{1,0:T(8,128)(2,1)S(1)}, u32[]{:S(2)}, u32[]{:S(2)}) %collective-permute-start.2) | collective-permute-done | bytes 196640 | tf_op jit(solution)/shard_map/ppermute | solution.py:53
  77.1 0.0 collective-permute-done.1.other_ref
  77.1 8.0 %head_grad.1 = bf16[7168,768]{1,0:T(8,128)(2,1)} custom-call(bf16[128,7168]{1,0:T(8,128)(2,1)} %get-tuple-element.23.own_ref, bf16[128,7168]{1,0:T(8,128)(2,1)} %collective-permute-done.1.other_ref, bf16[128,768]{1,0:T(8,128)(2,1)S(1)} %copy-done.1, bf16[128,768]{1,0:T(8,128)(2,1)S(1)} %collective-permute-done.2.other_grad_ref), custom_call_target="tpu_custom_call" | custom-call | flops 2818572288 | bytes 14680064 | tf_op jit(solution)/shard_map/head_grad/pallas_call | solution.py:313
  85.1 4.1 %all-to-all-done.3.part_ref = bf16[8,16,7168]{2,1,0:T(8,128)(2,1)S(1)} async-done(((bf16[8,16,7168]{2,1,0:T(8,128)(2,1)}), bf16[8,16,7168]{2,1,0:T(8,128)(2,1)S(1)}, u32[]{:S(2)}, u32[]{:S(2)}) %all-to-all-start.3) | async-done | bytes 1835040 | tf_op jit(solution)/shard_map/all_to_all | solution.py:47
  89.1 0.2 add_up.2
  89.4 0.1 reshape.27
  89.5 12.6 %all_to_all.28.part_ref = bf16[8,2,7168]{2,1,0:T(2,128)(2,1)S(1)} all-to-all(bf16[8,2,7168]{2,1,0:T(2,128)(2,1)S(1)} %reshape.27), channel_id=1, replica_groups={{0,1,4,5,8,9,12,13},{3,2,7,6,11,10,15,14},{68,69,64,65,76,77,72,73},{71..., dimensions={0} | all-to-all | bytes 458752 | tf_op jit(solution)/shard_map/all_to_all | solution.py:47
  102.1 0.7 add_up.3
  (9 shorter events, 0.0 us)
Async XLA Ops:
  0.6 43.5 %collective-permute-start = (bf16[7168,768]{1,0:T(8,128)(2,1)}, bf16[7168,768]{1,0:T(8,128)(2,1)S(1)}, u32[]{:S(2)}, u32[]{:S(2)}) collective-permute-start(bf16[7168,768]{1,0:T(8,128)(2,1)} %weight_ref.3), channel_id=1, source_target_pairs={{0,32},{32,0},{1,33},{33,1},{2,34},{34,2},{3,35},{35,3},{4,36},{36... | collective-permute-start | bytes 33030152 | tf_op jit(solution)/shard_map/ppermute | solution.py:53
  2.1 42.0 %copy-start = (bf16[7168,768]{1,0:T(8,128)(2,1)S(1)}, bf16[7168,768]{1,0:T(8,128)(2,1)}, u32[]{:S(2)}) copy-start(bf16[7168,768]{1,0:T(8,128)(2,1)} %weight_ref.3) | copy-start | bytes 33030148
  25.0 19.1 %copy-start.2 = (s32[256]{0:T(256)S(1)}, s32[256]{0:T(256)}, u32[]{:S(2)}) copy-start(s32[256]{0:T(256)} %param.9) | copy-start | bytes 3076
  25.0 19.1 %copy-start.3 = (s32[256]{0:T(256)S(1)}, s32[256]{0:T(256)}, u32[]{:S(2)}) copy-start(s32[256]{0:T(256)} %param.10) | copy-start | bytes 3076
  25.1 19.1 %copy-start.4 = (f32[256]{0:T(256)S(1)}, f32[256]{0:T(256)}, u32[]{:S(2)}) copy-start(f32[256]{0:T(256)} %param.11) | copy-start | bytes 3076
  60.9 16.1 %collective-permute-start.1 = (bf16[128,7168]{1,0:T(8,128)(2,1)}, bf16[128,7168]{1,0:T(8,128)(2,1)}, u32[]{:S(2)}, u32[]{:S(2)}) collective-permute-start(bf16[128,7168]{1,0:T(8,128)(2,1)} %get-tuple-element.23.own_ref), channel_id=1, source_target_pairs={{0,32},{32,0},{1,33},{33,1},{2,34},{34,2},{3,35},{35,3},{4,36},{36... | collective-permute-start | bytes 5505032 | tf_op jit(solution)/shard_map/ppermute | solution.py:53
  71.8 3.8 %copy-start.5 = (bf16[128,768]{1,0:T(8,128)(2,1)S(1)}, bf16[128,768]{1,0:T(8,128)(2,1)}, u32[]{:S(2)}) copy-start(bf16[128,768]{1,0:T(8,128)(2,1)} %get-tuple-element.25) | copy-start | bytes 589828
  71.8 5.3 %copy-start.1 = (bf16[128,768]{1,0:T(8,128)(2,1)S(1)}, bf16[128,768]{1,0:T(8,128)(2,1)}, u32[]{:S(2)}) copy-start(bf16[128,768]{1,0:T(8,128)(2,1)} %get-tuple-element.24.own_grad_ref) | copy-start | bytes 589828
  71.8 17.3 %all-to-all-start.3 = ((bf16[8,16,7168]{2,1,0:T(8,128)(2,1)}), bf16[8,16,7168]{2,1,0:T(8,128)(2,1)S(1)}, u32[]{:S(2)}, u32[]{:S(2)}) async-start(bf16[8,16,7168]{2,1,0:T(8,128)(2,1)} %bitcast.10), calls=%async_computation.3 | async-start | bytes 3670016 | tf_op jit(solution)/shard_map/all_to_all | solution.py:47
  75.6 1.5 %collective-permute-start.2 = (bf16[128,768]{1,0:T(8,128)(2,1)S(1)}, bf16[128,768]{1,0:T(8,128)(2,1)S(1)}, u32[]{:S(2)}, u32[]{:S(2)}) collective-permute-start(bf16[128,768]{1,0:T(8,128)(2,1)S(1)} %copy-done.5), channel_id=1, source_target_pairs={{0,32},{32,0},{1,33},{33,1},{2,34},{34,2},{3,35},{35,3},{4,36},{36... | collective-permute-start | bytes 589832 | tf_op jit(solution)/shard_map/ppermute | solution.py:53
